TPU v7x, 32 devices: a whole 2x2x4 slice. The times are simulated.
32 devices in a mesh: space: 4 (over y, x), species: 8 (over z, core).
Axes of the slice: x: 2, y: 2, z: 4, core: 2. Of those that a mesh axis runs over, the one named last changes fastest.
Arguments:
- dust_state: float32 [3, 32, 128, 1024], P(None, 'species', 'space'), may hold values from -4 to 4, as said below
- gas_state: float32 [3, 128, 1024], P(None, 'space'), may hold values from -2 to 2, as said below
- species_bin: int32 [32], P('species'), may hold values from 0 to 31, each once
Outputs:
- dust_out: float32 [3, 32, 128, 1024], P(None, 'species', 'space')
- gas_out: float32 [3, 128, 1024], P(None, 'space')
Inputs may be any that keep to these rules, and one draw needn't show every extreme that they name: `dust_state`: component 0 (densities) lies in 0.5 to 2; the velocities lie within -4 to 4. `gas_state`: component 0 (density) lies in 0.5 to 2; the velocities lie within -2 to 2.
All inputs are finite; a program needn't handle non-finite values.
Results may differ from a plain program's by a relative error of at most 0.0003.
Values sent between devices are 32-bit elements; how exact they have to be, the bound alone decides.
A program may use at most 64 MiB of HBM per device.

v0:
```python
import jax
import jax.numpy as jnp
from jax import lax
from jax.sharding import PartitionSpec as P

STEPS = 2


courant = 0.25
sound_speed = 1.0
sound_sq = 1.0
stop_floor = 0.003
stop_span = 6.907755


def padded(block, sides, width):
    for axis, dim in sides:
        count = lax.axis_size(axis)
        forward = [(i, i + 1) for i in range(count - 1)]
        forward.append((count - 1, 0))
        backward = [(target, source) for source, target in forward]
        low = lax.ppermute(
            lax.slice_in_dim(block, block.shape[dim] - width, None, axis=dim), axis, forward
        )
        high = lax.ppermute(lax.slice_in_dim(block, 0, width, axis=dim), axis, backward)
        block = jnp.concatenate([low, block, high], axis=dim)
    return block


def window(values, start, length, along):
    return lax.slice_in_dim(values, start, start + length, axis=along)


def face_divergence(density, velocity, along):
    faces = density.shape[along] - 3
    back_two = window(density, 0, faces, along)
    here = window(density, 1, faces, along)
    ahead = window(density, 2, faces, along)
    ahead_two = window(density, 3, faces, along)
    face_speed = 0.5 * (window(velocity, 1, faces, along) + window(velocity, 2, faces, along))
    flux = jnp.maximum(face_speed, 0.0) * (1.5 * here - 0.5 * back_two) + jnp.minimum(
        face_speed, 0.0
    ) * (1.5 * ahead - 0.5 * ahead_two)
    return window(flux, 1, faces - 1, along) - window(flux, 0, faces - 1, along)


def moved(fluid, step_time):
    density = fluid[0]
    radial = fluid[1]
    azimuth = fluid[2]
    div_azimuth = face_divergence(density, azimuth, 1)
    inner_density = density[:, 2:-2]
    inner_radial = radial[:, 2:-2]
    zero_pad = ((0, 0), (0, 0), (2, 2))
    div_radial = face_divergence(
        jnp.pad(inner_density, zero_pad), jnp.pad(inner_radial, zero_pad), 2
    )
    new_density = inner_density - step_time * (div_azimuth + div_radial)
    gas_density = density[-1]
    inner_gas = gas_density[2:-2]
    grad_azimuth = 0.5 * (gas_density[3:-1] - gas_density[1:-3])
    edge_gas = jnp.pad(inner_gas, ((0, 0), (1, 1)), mode="edge")
    grad_radial = 0.5 * (edge_gas[:, 2:] - edge_gas[:, :-2])
    push = step_time * sound_sq / inner_gas
    gas_velocity = jnp.stack(
        [inner_radial[-1] - push * grad_radial, azimuth[-1, 2:-2] - push * grad_azimuth]
    )
    dust_velocity = jnp.stack([inner_radial[:-1], azimuth[:-1, 2:-2]])
    return (new_density, gas_velocity, dust_velocity)


def drag_terms(new_density, dust_velocity, stop_times, step_time, total_species):
    gas_new = new_density[-1]
    rate = step_time * gas_new[None] / stop_times[:, None, None]
    weight = new_density[:-1] / (total_species * gas_new[None]) * rate / (1.0 + rate)
    terms = jnp.stack(
        [
            jnp.sum(weight, 0),
            jnp.sum(weight * dust_velocity[0], 0),
            jnp.sum(weight * dust_velocity[1], 0),
        ]
    )
    return (rate, terms)


def coupled_gas(gas_velocity, totals):
    return (gas_velocity + totals[1:]) / (1.0 + totals[0])


def assemble(new_density, dust_velocity, gas_next, rate):
    dust_next = (dust_velocity + rate[None] * gas_next[:, None]) / (1.0 + rate[None])
    radial = jnp.concatenate([dust_next[0], gas_next[0][None]], axis=0)
    azimuth = jnp.concatenate([dust_next[1], gas_next[1][None]], axis=0)
    return jnp.stack([new_density, radial, azimuth])


def advance(wide, margin, tile_rows, stop_times, total_species):
    interior = lax.slice_in_dim(wide, margin, margin + tile_rows, axis=2)
    local_top = jnp.max(jnp.abs(interior[1]) + jnp.abs(interior[2]))
    fastest = lax.pmax(local_top, ("space", "species"))
    step_time = courant / (sound_speed + fastest)
    new_density, gas_velocity, dust_velocity = moved(wide, step_time)
    rate, terms = drag_terms(new_density, dust_velocity, stop_times, step_time, total_species)
    totals = lax.psum(terms, "species")
    gas_next = coupled_gas(gas_velocity, totals)
    return assemble(new_density, dust_velocity, gas_next, rate)


def local(dust_state, gas_state, species_bin):
    local_species = dust_state.shape[1]
    total_species = local_species * lax.axis_size("species")
    tile_rows = dust_state.shape[2]
    fluid = jnp.concatenate([dust_state, gas_state[:, None]], axis=1)
    stop_times = stop_floor * jnp.exp(
        stop_span * species_bin.astype(jnp.float32) / (total_species - 1)
    )
    for iteration in range(STEPS):
        wide = padded(fluid, (("space", 2),), 2)
        fluid = advance(wide, 2, tile_rows, stop_times, total_species)
    return (fluid[:, :local_species], fluid[:, local_species])


def solution(mesh):
    placed = (P(None, "species", "space", None), P(None, "space", None), P("species"))
    return jax.shard_map(
        local,
        mesh=mesh,
        in_specs=placed,
        out_specs=(P(None, "species", "space", None), P(None, "space", None)),
        check_vma=False,
    )
```

profile of v0, /device:TPU:0, one launch (start us, length us, event | category | flops | bytes accessed | tf_op | source)
XLA Modules:
  0.0 237.9 jit_solution(12726010728612844711)
XLA Ops:
  7.2 1.4 pad_maximum_fusion.26
  8.7 3.0 %collective-permute-start = (f32[3,5,2,1024]{3,2,1,0:T(2,128)S(1)}, f32[3,5,2,1024]{3,2,1,0:T(2,128)S(1)}, u32[]{:S(2)}, u32[]{:S(2)}) collective-permute-start(f32[3,5,2,1024]{3,2,1,0:T(2,128)S(1)} %get-tuple-element.18), channel_id=1, source_target_pairs={{0,8},{8,16},{16,24},{24,0},{1,9},{9,17},{17,25},{25,1},{2,10},{10... | collective-permute-start | bytes 368648 | tf_op jit(solution)/shard_map/ppermute | solution.py:22
  12.4 1.2 collective-permute-start.1
  13.6 40.1 %pmax.14 = f32[]{:T(128)} all-reduce(f32[]{:T(128)} %fusion.22), channel_id=1, replica_groups=mesh['space'=4,'species'=8] {'space','species'}, use_global_device_ids=true, to_apply=%region_1.0 | all-reduce | flops 1 | bytes 8 | tf_op jit(solution)/shard_map/pmax | solution.py:100
  56.0 0.8 multiply_add_fusion.1
  57.4 1.0 fusion.54
  59.5 56.3 %all-reduce.7.cloned.1.call-done = f32[3,32,1024]{2,1,0:T(8,128)} async-done(((f32[3,32,1024]{2,1,0:T(8,128)}), f32[3,32,1024]{2,1,0:T(8,128)}) %all-reduce.7.cloned.1.call-update) | async-done | bytes 393232 | tf_op jit(solution)/shard_map/psum | solution.py:104
  115.8 0.9 fusion.42
  116.7 1.0 fusion.30
  117.7 1.3 fusion
  119.1 0.9 add_reduce_fusion
  120.0 1.5 collective-permute-start.2
  121.5 1.5 collective-permute-start.3
  123.1 38.5 %pmax.15 = f32[]{:T(128)} all-reduce(f32[]{:T(128)} %get-tuple-element.30), channel_id=1, replica_groups=mesh['space'=4,'species'=8] {'space','species'}, use_global_device_ids=true, to_apply=%region_7.8 | all-reduce | flops 1 | bytes 8 | tf_op jit(solution)/shard_map/pmax | solution.py:100
  163.8 0.8 multiply_add_fusion
  165.0 1.2 broadcast_divide_fusion
  166.2 1.2 fusion.53
  168.2 1.9 fusion.41
  170.1 1.4 fusion.36
  171.6 53.2 %all-reduce.9.cloned.1.call-done = f32[3,32,1024]{2,1,0:T(8,128)} async-done(((f32[3,32,1024]{2,1,0:T(8,128)}), f32[3,32,1024]{2,1,0:T(8,128)}) %all-reduce.9.cloned.1.call-update) | async-done | bytes 393232 | tf_op jit(solution)/shard_map/psum | solution.py:104
  224.7 0.9 fusion.31
  225.7 1.1 fusion.29
  226.8 1.7 fusion.1
  229.8 1.2 copy.7
  (55 shorter events, 8.1 us)
Async XLA Ops:
  7.2 4.5 %copy-start = (f32[3,4,32,1024]{3,2,1,0:T(8,128)S(1)}, f32[3,4,32,1024]{3,2,1,0:T(8,128)}, u32[]{:S(2)}) copy-start(f32[3,4,32,1024]{3,2,1,0:T(8,128)} %param.3) | copy-start | bytes 4718596
  7.2 4.5 %copy-start.1 = (f32[3,32,1024]{2,1,0:T(8,128)S(1)}, f32[3,32,1024]{2,1,0:T(8,128)}, u32[]{:S(2)}) copy-start(f32[3,32,1024]{2,1,0:T(8,128)} %param.4) | copy-start | bytes 1179652
  7.2 47.2 %copy-start.6 = (s32[4]{0:T(128)S(1)}, s32[4]{0:T(128)}, u32[]{:S(2)}) copy-start(s32[4]{0:T(128)} %param.5) | copy-start | bytes 52
  7.2 108.6 %all-reduce.7.cloned.1.call-start = ((), (), s32[]{:S(2)}) async-start(), calls=%async_computation | async-start | bytes 786432 | tf_op jit(solution)/shard_map/psum | solution.py:104
  8.7 45.8 %collective-permute-start = (f32[3,5,2,1024]{3,2,1,0:T(2,128)S(1)}, f32[3,5,2,1024]{3,2,1,0:T(2,128)S(1)}, u32[]{:S(2)}, u32[]{:S(2)}) collective-permute-start(f32[3,5,2,1024]{3,2,1,0:T(2,128)S(1)} %get-tuple-element.18), channel_id=1, source_target_pairs={{0,8},{8,16},{16,24},{24,0},{1,9},{9,17},{17,25},{25,1},{2,10},{10... | collective-permute-start | bytes 368648 | tf_op jit(solution)/shard_map/ppermute | solution.py:22
  12.4 42.0 %collective-permute-start.1 = (f32[3,5,2,1024]{3,2,1,0:T(2,128)S(1)}, f32[3,5,2,1024]{3,2,1,0:T(2,128)S(1)}, u32[]{:S(2)}, u32[]{:S(2)}) collective-permute-start(f32[3,5,2,1024]{3,2,1,0:T(2,128)S(1)} %get-tuple-element.19), channel_id=1, source_target_pairs={{8,0},{16,8},{24,16},{0,24},{9,1},{17,9},{25,17},{1,25},{10,2},{18... | collective-permute-start | bytes 368648 | tf_op jit(solution)/shard_map/ppermute | solution.py:25
  59.2 165.5 %all-reduce.9.cloned.1.call-start = ((), (), s32[]{:S(2)}) async-start(), calls=%async_computation.1 | async-start | bytes 786432 | tf_op jit(solution)/shard_map/psum | solution.py:104
  59.5 63.5 %copy-start.3 = (f32[32,1024]{1,0:T(8,128)}, f32[32,1024]{1,0:T(8,128)S(1)}, u32[]{:S(2)}) copy-start(f32[32,1024]{1,0:T(8,128)S(1)} %slice_bitcast_fusion.16) | copy-start | bytes 393220
  120.0 42.3 %collective-permute-start.2 = (f32[3,5,2,1024]{3,2,1,0:T(2,128)S(1)}, f32[3,5,2,1024]{3,2,1,0:T(2,128)S(1)}, u32[]{:S(2)}, u32[]{:S(2)}) collective-permute-start(f32[3,5,2,1024]{3,2,1,0:T(2,128)S(1)} %get-tuple-element.16), channel_id=1, source_target_pairs={{0,8},{8,16},{16,24},{24,0},{1,9},{9,17},{17,25},{25,1},{2,10},{10... | collective-permute-start | bytes 368648 | tf_op jit(solution)/shard_map/ppermute | solution.py:22
  121.5 40.8 %collective-permute-start.3 = (f32[3,5,2,1024]{3,2,1,0:T(2,128)S(1)}, f32[3,5,2,1024]{3,2,1,0:T(2,128)S(1)}, u32[]{:S(2)}, u32[]{:S(2)}) collective-permute-start(f32[3,5,2,1024]{3,2,1,0:T(2,128)S(1)} %get-tuple-element.17), channel_id=1, source_target_pairs={{8,0},{16,8},{24,16},{0,24},{9,1},{17,9},{25,17},{1,25},{10,2},{18... | collective-permute-start | bytes 368648 | tf_op jit(solution)/shard_map/ppermute | solution.py:25
  162.3 0.7 copy-start.4
  162.3 0.7 copy-start.5
  163.0 3.2 %copy-start.2 = (f32[5,36,1024]{2,1,0:T(8,128)}, f32[5,36,1024]{2,1,0:T(8,128)S(1)}, u32[]{:S(2)}) copy-start(f32[5,36,1024]{2,1,0:T(8,128)S(1)} %get-tuple-element.11) | copy-start | bytes 2211844
Sparse Core Ops, SparseCore 0:
  59.4 56.3 all-reduce.6
  168.3 56.3 all-reduce.8
where the time goes:
time: 239 us; the launch traced here: 238 us
  waiting for transfers between devices  110 us (46%)
  blocking collectives  78.6 us (33%)
  other arithmetic  24.2 us (10%)
  between operations  15.8 us (7%)
  starting transfers between devices  7.23 us (3%)
  local copies, waits for them, and re-layouts  2.58 us (1%)
    psum x2, waiting for transfers between devices, advance(): totals = lax.psum(terms, 'species')  109 us
    pmax x2, blocking collectives, advance(): fastest = lax.pmax(local_top, ('space', 'species'))  78.6 us
  transfers between devices with their start and end apart: 6, of which 2 were waited for; matrix products, arithmetic and copies ran while one was open for 2% of the time, Pallas kernels for 0%

commit v1 on v0

v1 whole, which is shorter than its diff:
```python
import functools

import jax
import jax.numpy as jnp
from jax import lax
from jax.experimental import pallas as pl
from jax.experimental.pallas import tpu as pltpu
from jax.sharding import PartitionSpec as P

STEPS = 2

courant = 0.25
sound_speed = 1.0
stop_floor = 0.003
stop_span = 6.907755

MESH = pl.DeviceIdType.MESH
TOP = 8


def kernel(
    n, m, dust, gas, inv_stop, dust_out, gas_out,
    rho, rad, azi, div, push, damp, terms, gnew,
    sib_recv, rs_recv, top_send, top_one, top_mid, top_two, halo_send, halo_recv,
    io_sem, top_sems, halo_sems, sib_sems, rs_sems, ag_sems, fw_sems,
):
    local_species, tile_rows, cells = dust.shape[1:]
    fluids = local_species + 1
    gas_at = local_species
    groups = tile_rows // 8
    spans = n // groups
    width = cells // spans
    chips = n // 2
    total_species = local_species * n
    bottom = TOP + tile_rows

    me_space = lax.axis_index("space")
    me = lax.axis_index("species")
    core = lax.rem(me, 2)
    chip = me // 2
    sibling = me + 1 - 2 * core
    interior = pl.ds(TOP, tile_rows)

    loads = []
    for part, held in enumerate((rho, rad, azi)):
        loads.append(pltpu.make_async_copy(
            dust.at[part], held.at[pl.ds(0, local_species), interior], io_sem.at[2 * part]))
        loads.append(pltpu.make_async_copy(
            gas.at[part], held.at[gas_at, interior], io_sem.at[2 * part + 1]))
    for load in loads:
        load.start()

    barrier = pltpu.get_barrier_semaphore()

    def greet_species(i, carry):
        pl.semaphore_signal(
            barrier, inc=1, device_id=(me_space, lax.rem(me + 1 + i, n)), device_id_type=MESH)
        return carry

    def greet_space(i, carry):
        pl.semaphore_signal(
            barrier, inc=1, device_id=(lax.rem(me_space + 1 + i, m), me), device_id_type=MESH)
        return carry

    lax.fori_loop(0, n - 1, greet_species, 0)
    lax.fori_loop(0, m - 1, greet_space, 0)
    for load in loads:
        load.wait()

    def fold(values):
        best = values[:, :128]
        for start in range(128, values.shape[1], 128):
            best = jnp.maximum(best, values[:, start:start + 128])
        return best

    def first_top(i, best):
        f = i // groups
        rows = pl.ds(pl.multiple_of(TOP + 8 * lax.rem(i, groups), 8), 8)
        return jnp.maximum(best, fold(jnp.abs(rad[f, rows, :]) + jnp.abs(azi[f, rows, :])))

    top = lax.fori_loop(0, fluids * groups, first_top, jnp.zeros((8, 128), jnp.float32))

    def copy_to(src, dst, send, recv, where):
        return pltpu.make_async_remote_copy(
            src_ref=src, dst_ref=dst, send_sem=send, recv_sem=recv,
            device_id=where, device_id_type=MESH)

    lanes = lax.broadcasted_iota(jnp.int32, (8, cells), 1)

    for step in range(STEPS):
        top_send[step] = top
        top_one[step, me] = top
        for f in range(fluids):
            for side, (far, near) in enumerate(((bottom - 2, bottom - 1), (TOP + 1, TOP))):
                halo_send[step, side, f:f + 1, :] = rho[f, far:far + 1, :]
                halo_send[step, side, fluids + f:fluids + f + 1, :] = rho[f, near:near + 1, :]
                halo_send[step, side, 2 * fluids + f:2 * fluids + f + 1, :] = azi[f, near:near + 1, :]
        if step == 0:
            pl.semaphore_wait(barrier, n + m - 2)

        def top_copy_one(i):
            there = lax.rem(me + 1 + i, n)
            return copy_to(top_send.at[step], top_one.at[step, me], top_sems.at[step, 0, i],
                           top_sems.at[step, 1, me], (me_space, there))

        def top_copy_two(i):
            there = lax.rem(me_space + 1 + i, m)
            return copy_to(top_mid.at[step], top_two.at[step, me_space], top_sems.at[step, 2, i],
                           top_sems.at[step, 3, me_space], (there, me))

        def start_one(i, carry):
            top_copy_one(i).start()
            return carry

        lax.fori_loop(0, n - 1, start_one, 0)
        halos = []
        for side, there in enumerate((lax.rem(me_space + 1, m), lax.rem(me_space + m - 1, m))):
            halos.append(copy_to(halo_send.at[step, side], halo_recv.at[step, side],
                                 halo_sems.at[step, 0, side], halo_sems.at[step, 1, side],
                                 (there, me)))
        for halo in halos:
            halo.start()

        def radial(i, carry):
            f = i // groups
            r = lax.rem(i, groups)
            rows = pl.ds(pl.multiple_of(TOP + 8 * r, 8), 8)
            here = rho[f, rows, :]
            speed = rad[f, rows, :]
            back = jnp.where(lanes >= 1, pltpu.roll(here, 1, 1), 0.0)
            ahead = jnp.where(lanes < cells - 1, pltpu.roll(here, cells - 1, 1), 0.0)
            down = 3.0 * here - ahead
            down_next = jnp.where(lanes < cells - 1, pltpu.roll(down, cells - 1, 1), 0.0)
            face = speed + jnp.where(lanes < cells - 1, pltpu.roll(speed, cells - 1, 1), 0.0)
            flux = face * jnp.where(face > 0.0, 3.0 * here - back, down_next)
            before = jnp.where(lanes >= 1, pltpu.roll(flux, 1, 1), jnp.minimum(speed, 0.0) * down)
            div[f, pl.ds(pl.multiple_of(8 * r, 8), 8), :] = flux - before
            return carry

        lax.fori_loop(0, fluids * groups, radial, 0)

        def gas_push(r, carry):
            rows = pl.ds(pl.multiple_of(TOP + 8 * r, 8), 8)
            here = rho[gas_at, rows, :]
            up = jnp.where(lanes < cells - 1, pltpu.roll(here, cells - 1, 1), here)
            low = jnp.where(lanes >= 1, pltpu.roll(here, 1, 1), here)
            push[0, pl.ds(pl.multiple_of(8 * r, 8), 8), :] = (up - low) * (0.5 / here)
            return carry

        lax.fori_loop(0, groups, gas_push, 0)

        def wait_one(i, best):
            there = lax.rem(me + 1 + i, n)
            copy_to(top_send.at[step], top_one.at[step, there], top_sems.at[step, 0, i],
                    top_sems.at[step, 1, there], (me_space, there)).wait_recv()
            return jnp.maximum(best, top_one[step, there])

        top = lax.fori_loop(0, n - 1, wait_one, top)
        top_mid[step] = top

        def start_two(i, carry):
            top_copy_two(i).start()
            return carry

        lax.fori_loop(0, m - 1, start_two, 0)

        for halo in halos:
            halo.wait_recv()
        for f in range(fluids):
            for side, (far, near) in enumerate(((TOP - 2, TOP - 1), (bottom + 1, bottom))):
                rho[f, far:far + 1, :] = halo_recv[step, side, f:f + 1, :]
                rho[f, near:near + 1, :] = halo_recv[step, side, fluids + f:fluids + f + 1, :]
                azi[f, near:near + 1, :] = halo_recv[
                    step, side, 2 * fluids + f:2 * fluids + f + 1, :]

        def azimuthal(f, carry):
            for r in range(groups):
                at = TOP + 8 * r
                here = rho[f, at:at + 8, :]
                back_two = rho[f, at - 2:at + 6, :]
                back = rho[f, at - 1:at + 7, :]
                ahead = rho[f, at + 1:at + 9, :]
                ahead_two = rho[f, at + 2:at + 10, :]
                speed = azi[f, at:at + 8, :]
                low = speed + azi[f, at - 1:at + 7, :]
                high = speed + azi[f, at + 1:at + 9, :]
                after = high * jnp.where(high > 0.0, 3.0 * here - back, 3.0 * ahead - ahead_two)
                before = low * jnp.where(low > 0.0, 3.0 * back - back_two, 3.0 * here - ahead)
                div[f, 8 * r:8 * r + 8, :] += after - before
            return carry

        lax.fori_loop(0, fluids, azimuthal, 0)
        for r in range(groups):
            at = TOP + 8 * r
            push[1, 8 * r:8 * r + 8, :] = (
                rho[gas_at, at + 1:at + 9, :] - rho[gas_at, at - 1:at + 7, :]
            ) * (0.5 / rho[gas_at, at:at + 8, :])

        def wait_two(i, best):
            there = lax.rem(me_space + 1 + i, m)
            copy_to(top_mid.at[step], top_two.at[step, there], top_sems.at[step, 2, i],
                    top_sems.at[step, 3, there], (there, me)).wait_recv()
            return jnp.maximum(best, top_two[step, there])

        top = lax.fori_loop(0, m - 1, wait_two, top)
        fastest = jnp.max(jnp.max(top, axis=0, keepdims=True), axis=1, keepdims=True)
        dt = courant / (sound_speed + fastest)
        dt_quarter = 0.25 * dt

        def place(chunk):
            r = chunk // spans
            g = lax.rem(chunk, spans)
            cols = pl.ds(pl.multiple_of(width * g, 128), width)
            return (pl.ds(pl.multiple_of(TOP + 8 * r, 8), 8),
                    pl.ds(pl.multiple_of(8 * r, 8), 8), cols)

        def drag(chunk):
            rows, inner, cols = place(chunk)
            new_gas = rho[gas_at, rows, cols] - dt_quarter * div[gas_at, inner, cols]
            rho[gas_at, rows, cols] = new_gas
            sums = [jnp.zeros((8, width), jnp.float32)] * 3
            for k in range(local_species):
                scale = dt * inv_stop[k]
                new = rho[k, rows, cols] - dt_quarter * div[k, inner, cols]
                rho[k, rows, cols] = new
                factor = 1.0 / (1.0 + scale * new_gas)
                damp[k, inner, cols] = factor
                weight = (new * factor) * (scale * (1.0 / total_species))
                sums[0] = sums[0] + weight
                sums[1] = sums[1] + weight * rad[k, rows, cols]
                sums[2] = sums[2] + weight * azi[k, rows, cols]
            return sums

        def sib_copy(i):
            return copy_to(terms.at[step, 1 - core, i], sib_recv.at[step, i],
                           sib_sems.at[step, 0, i], sib_sems.at[step, 1, i], (me_space, sibling))

        def rs_copy(z):
            return copy_to(terms.at[step, core, z], rs_recv.at[step, chip],
                           rs_sems.at[step, 0, z], rs_sems.at[step, 1, chip],
                           (me_space, 2 * z + core))

        def rs_arrival(z):
            return copy_to(terms.at[step, core, z], rs_recv.at[step, z],
                           rs_sems.at[step, 0, z], rs_sems.at[step, 1, z],
                           (me_space, 2 * z + core))

        def for_sibling(i, carry):
            z = lax.rem(chip + 1 + i, chips)
            sums = drag(2 * z + 1 - core)
            for part in range(3):
                terms[step, 1 - core, z, part] = sums[part]
            sib_copy(z).start()
            return carry

        lax.fori_loop(0, chips, for_sibling, 0)

        def for_peers(i, carry):
            z = lax.rem(chip + 1 + i, chips)
            sums = drag(2 * z + core)
            sib_copy(z).wait_recv()
            for part in range(3):
                terms[step, core, z, part] = sums[part] + sib_recv[step, z, part]

            @pl.when(i < chips - 1)
            def _():
                rs_copy(z).start()

            return carry

        lax.fori_loop(0, chips, for_peers, 0)

        def gather_sums(i, sums):
            z = lax.rem(chip + 1 + i, chips)
            rs_arrival(z).wait_recv()
            return tuple(sums[part] + rs_recv[step, z, part] for part in range(3))

        sums = lax.fori_loop(
            0, chips - 1, gather_sums, tuple(terms[step, core, chip, part] for part in range(3)))

        rows, inner, cols = place(me)
        inverse = 1.0 / (1.0 + sums[0])
        gnew[step, me, 0] = (rad[gas_at, rows, cols] - dt * push[0, inner, cols] + sums[1]) * inverse
        gnew[step, me, 1] = (azi[gas_at, rows, cols] - dt * push[1, inner, cols] + sums[2]) * inverse

        def ag_copy(z):
            return copy_to(gnew.at[step, me], gnew.at[step, me], ag_sems.at[step, 0, z],
                           ag_sems.at[step, 1, chip], (me_space, 2 * z + core))

        def ag_arrival(z):
            return copy_to(gnew.at[step, 2 * z + core], gnew.at[step, 2 * z + core],
                           ag_sems.at[step, 0, z], ag_sems.at[step, 1, z],
                           (me_space, 2 * z + core))

        def fw_copy(z):
            return copy_to(gnew.at[step, 2 * z + core], gnew.at[step, 2 * z + core],
                           fw_sems.at[step, 0, z], fw_sems.at[step, 1, z], (me_space, sibling))

        def fw_arrival(z):
            other = 2 * z + 1 - core
            return copy_to(gnew.at[step, other], gnew.at[step, other],
                           fw_sems.at[step, 0, z], fw_sems.at[step, 1, z], (me_space, sibling))

        def start_ag(i, carry):
            ag_copy(lax.rem(chip + 1 + i, chips)).start()
            return carry

        lax.fori_loop(0, chips - 1, start_ag, 0)
        fw_copy(chip).start()

        def update(chunk, best):
            rows, inner, cols = place(chunk)
            gas_rad = gnew[step, chunk, 0]
            gas_azi = gnew[step, chunk, 1]
            rad[gas_at, rows, cols] = gas_rad
            azi[gas_at, rows, cols] = gas_azi
            speed = jnp.abs(gas_rad) + jnp.abs(gas_azi)
            for k in range(local_species):
                factor = damp[k, inner, cols]
                new_rad = gas_rad + (rad[k, rows, cols] - gas_rad) * factor
                new_azi = gas_azi + (azi[k, rows, cols] - gas_azi) * factor
                rad[k, rows, cols] = new_rad
                azi[k, rows, cols] = new_azi
                speed = jnp.maximum(speed, jnp.abs(new_rad) + jnp.abs(new_azi))
            return jnp.maximum(best, fold(speed))

        top = update(me, jnp.zeros((8, 128), jnp.float32))

        def update_peer(i, best):
            z = lax.rem(chip + 1 + i, chips)
            ag_arrival(z).wait_recv()
            fw_copy(z).start()
            return update(2 * z + core, best)

        top = lax.fori_loop(0, chips - 1, update_peer, top)

        def update_sibling(i, best):
            z = lax.rem(chip + i, chips)
            fw_arrival(z).wait_recv()
            return update(2 * z + 1 - core, best)

        top = lax.fori_loop(0, chips, update_sibling, top)

        def sent_one(i, carry):
            top_copy_one(i).wait_send()
            return carry

        def sent_two(i, carry):
            top_copy_two(i).wait_send()
            return carry

        def sent_core(i, carry):
            sib_copy(i).wait_send()
            fw_copy(i).wait_send()
            return carry

        def sent_chip(i, carry):
            z = lax.rem(chip + 1 + i, chips)
            rs_copy(z).wait_send()
            ag_copy(z).wait_send()
            return carry

        lax.fori_loop(0, n - 1, sent_one, 0)
        lax.fori_loop(0, m - 1, sent_two, 0)
        lax.fori_loop(0, chips, sent_core, 0)
        lax.fori_loop(0, chips - 1, sent_chip, 0)
        for halo in halos:
            halo.wait_send()

    stores = []
    for part, held in enumerate((rho, rad, azi)):
        stores.append(pltpu.make_async_copy(
            held.at[pl.ds(0, local_species), interior], dust_out.at[part], io_sem.at[2 * part]))
        stores.append(pltpu.make_async_copy(
            held.at[gas_at, interior], gas_out.at[part], io_sem.at[2 * part + 1]))
    for store in stores:
        store.start()
    for store in stores:
        store.wait()


def solution(mesh):
    n = mesh.shape["species"]
    m = mesh.shape["space"]

    def local(dust_state, gas_state, species_bin):
        local_species, tile_rows, cells = dust_state.shape[1:]
        fluids = local_species + 1
        groups = tile_rows // 8
        width = cells // (n // groups)
        chips = n // 2
        total_species = local_species * n
        inv_stop = jnp.exp(
            -stop_span * species_bin.astype(jnp.float32) / (total_species - 1)
        ) / stop_floor
        f32 = jnp.float32
        halo_rows = -(-3 * fluids // 8) * 8
        extended = pltpu.VMEM((fluids, tile_rows + 16, cells), f32)
        dma = pltpu.SemaphoreType.DMA
        return pl.pallas_call(
            functools.partial(kernel, n, m),
            out_shape=(jax.ShapeDtypeStruct(dust_state.shape, f32),
                       jax.ShapeDtypeStruct(gas_state.shape, f32)),
            in_specs=[pl.BlockSpec(memory_space=pl.ANY), pl.BlockSpec(memory_space=pl.ANY),
                      pl.BlockSpec(memory_space=pltpu.SMEM)],
            out_specs=(pl.BlockSpec(memory_space=pl.ANY), pl.BlockSpec(memory_space=pl.ANY)),
            scratch_shapes=[
                extended, extended, extended,
                pltpu.VMEM((fluids, tile_rows, cells), f32),
                pltpu.VMEM((2, tile_rows, cells), f32),
                pltpu.VMEM((local_species, tile_rows, cells), f32),
                pltpu.VMEM((STEPS, 2, chips, 3, 8, width), f32),
                pltpu.VMEM((STEPS, n, 2, 8, width), f32),
                pltpu.VMEM((STEPS, chips, 3, 8, width), f32),
                pltpu.VMEM((STEPS, chips, 3, 8, width), f32),
                pltpu.VMEM((STEPS, 8, 128), f32),
                pltpu.VMEM((STEPS, n, 8, 128), f32),
                pltpu.VMEM((STEPS, 8, 128), f32),
                pltpu.VMEM((STEPS, m, 8, 128), f32),
                pltpu.VMEM((STEPS, 2, halo_rows, cells), f32),
                pltpu.VMEM((STEPS, 2, halo_rows, cells), f32),
                dma((6,)),
                dma((STEPS, 4, max(n, m))),
                dma((STEPS, 2, 2)),
                dma((STEPS, 2, chips)),
                dma((STEPS, 2, chips)),
                dma((STEPS, 2, chips)),
                dma((STEPS, 2, chips)),
            ],
            compiler_params=pltpu.CompilerParams(
                collective_id=0, has_side_effects=True, vmem_limit_bytes=56 * 1024 * 1024),
            cost_estimate=pl.CostEstimate(
                flops=200 * fluids * tile_rows * cells,
                bytes_accessed=24 * fluids * tile_rows * cells, transcendentals=0),
            name="disk_steps",
        )(dust_state, gas_state, inv_stop)

    return jax.shard_map(
        local,
        mesh=mesh,
        in_specs=(P(None, "species", "space", None), P(None, "space", None), P("species")),
        out_specs=(P(None, "species", "space", None), P(None, "space", None)),
        check_vma=False,
    )
```

time: 239 us -> 54.9 us (0.23)
  waiting for transfers between devices: 110 us -> 0 us
  blocking collectives: 78.6 us -> 0 us
  Pallas kernels: 0 us -> 49.3 us
  other arithmetic: 24.2 us -> 1.18 us
  between operations: 15.8 us -> 0.65 us
  starting transfers between devices: 7.23 us -> 0 us
    psum x2 -> x0, waiting for transfers between devices: 109 us -> none  [advance(): totals = lax.psum(terms, 'species')]
    pmax x2 -> x0, blocking collectives: 78.6 us -> none  [advance(): fastest = lax.pmax(local_top, ('space', 'species'))]
    pallas_call x0 -> x1, Pallas kernels: none -> 49.3 us  [local(): pl.pallas_call(functools.partial(kernel, n, m), out_shape=(jax.ShapeDtype...]
    div x10 -> x1, other arithmetic: 8.36 us -> 1.18 us  [local(): jnp.exp(-stop_span * species_bin.astype(jnp.float32) / (total_species - 1))]
    ppermute x4 -> x0, starting transfers between devices: 7.15 us -> none  [the longest x2 4.51 us: padded(): lax.ppermute(lax.slice_in_dim(block, block.shape[dim] - width, None, axis...]
    another operation x6 -> x0, other arithmetic: 3.88 us -> none  [the longest x2 2.04 us: moved(): jnp.stack([inner_radial[-1] - push * grad_radial, azimuth[-1, 2:-2] - pus...]
    add x4 -> x0, other arithmetic: 2.84 us -> none  [face_divergence(): jnp.maximum(face_speed, 0.0) * (1.5 * here - 0.5 * back_two)]
  transfers between devices with their start and end apart: 6 -> 0, of which waited for: 2 -> 0; matrix products, arithmetic and copies ran while one was open for 2% -> 0% of each run, Pallas kernels for 0% -> 0%
where the time goes in v1:
time: 54.9 us; the launch traced here: 54.7 us
  Pallas kernels  49.3 us (90%)
  local copies, waits for them, and re-layouts  3.53 us (6%)
  other arithmetic  1.18 us (2%)
  between operations  0.65 us (1%)
    pallas_call x1, Pallas kernels, local(): pl.pallas_call(functools.partial(kernel, n, m), out_shape=(jax.ShapeDtype...  49.3 us
    unnamed x4, local copies, waits for them, and re-layouts  3.53 us
    div x1, other arithmetic, local(): jnp.exp(-stop_span * species_bin.astype(jnp.float32) / (total_species - 1))  1.18 us

profile of v1, /device:TPU:0, one launch (start us, length us, event | category | flops | bytes accessed | tf_op | source)
XLA Modules:
  0.0 54.7 jit_solution(2054900580562577522)
XLA Ops:
  0.6 1.2 %exponential_multiply_fusion.inv_stop = f32[4]{0:T(128)} fusion(s32[4]{0:T(128)} %param.5), kind=kLoop, calls=%fused_computation | loop fusion | flops 12 | bytes 32 | tf_op jit(solution)/shard_map/div | solution.py:393
  1.8 49.3 %disk_steps.1 = (f32[3,4,32,1024]{3,2,1,0:T(8,128)}, f32[3,32,1024]{2,1,0:T(8,128)}) custom-call(f32[3,4,32,1024]{3,2,1,0:T(8,128)} %dust.1, f32[3,32,1024]{2,1,0:T(8,128)} %gas.1, f32[4]{0:T(128)} %exponential_multiply_fusion.inv_stop), custom_call_target="tpu_custom_call" | custom-call | flops 32768000 | bytes 3932160 | tf_op jit(solution)/shard_map/disk_steps/pallas_call | solution.py:400
  51.1 0.0 copy-start
  51.1 2.8 %copy.7 = f32[3,4,32,1024]{3,2,1,0:T(8,128)} copy(f32[3,4,32,1024]{3,2,1,0:T(8,128)} %get-tuple-element.4) | data formatting | bytes 3145728
  53.9 0.0 copy-done
  53.9 0.7 %copy.8 = f32[3,32,1024]{2,1,0:T(8,128)} copy(f32[3,32,1024]{2,1,0:T(8,128)S(1)} %copy-done) | data formatting | bytes 786432
Async XLA Ops:
  51.1 2.8 %copy-start = (f32[3,32,1024]{2,1,0:T(8,128)S(1)}, f32[3,32,1024]{2,1,0:T(8,128)}, u32[]{:S(2)}) copy-start(f32[3,32,1024]{2,1,0:T(8,128)} %get-tuple-element.5) | copy-start | bytes 1179652

commit v2 on v1

--- a/solution.py
+++ b/solution.py
@@ -19,8 +19,8 @@
 
 
 def kernel(
-    n, m, dust, gas, inv_stop, dust_out, gas_out,
-    rho, rad, azi, div, push, damp, terms, gnew,
+    n, m, dust, gas, species_bins, rho, rad, azi, damp,
+    species_bin, div, push, terms, gnew,
     sib_recv, rs_recv, top_send, top_one, top_mid, top_two, halo_send, halo_recv,
     io_sem, top_sems, halo_sems, sib_sems, rs_sems, ag_sems, fw_sems,
 ):
@@ -41,29 +41,29 @@
     sibling = me + 1 - 2 * core
     interior = pl.ds(TOP, tile_rows)
 
+    barrier = pltpu.get_barrier_semaphore()
+
+    def greet_species(i, carry):
+        pl.semaphore_signal(
+            barrier, inc=1, device_id=(me_space, lax.rem(me + 1 + i, n)), device_id_type=MESH)
+        return carry
+
+    def greet_space(i, carry):
+        pl.semaphore_signal(
+            barrier, inc=1, device_id=(lax.rem(me_space + 1 + i, m), me), device_id_type=MESH)
+        return carry
+
+    lax.fori_loop(0, n - 1, greet_species, 0)
+    lax.fori_loop(0, m - 1, greet_space, 0)
     loads = []
     for part, held in enumerate((rho, rad, azi)):
         loads.append(pltpu.make_async_copy(
             dust.at[part], held.at[pl.ds(0, local_species), interior], io_sem.at[2 * part]))
         loads.append(pltpu.make_async_copy(
             gas.at[part], held.at[gas_at, interior], io_sem.at[2 * part + 1]))
+    loads.append(pltpu.make_async_copy(species_bins, species_bin, io_sem.at[6]))
     for load in loads:
         load.start()
-
-    barrier = pltpu.get_barrier_semaphore()
-
-    def greet_species(i, carry):
-        pl.semaphore_signal(
-            barrier, inc=1, device_id=(me_space, lax.rem(me + 1 + i, n)), device_id_type=MESH)
-        return carry
-
-    def greet_space(i, carry):
-        pl.semaphore_signal(
-            barrier, inc=1, device_id=(lax.rem(me_space + 1 + i, m), me), device_id_type=MESH)
-        return carry
-
-    lax.fori_loop(0, n - 1, greet_species, 0)
-    lax.fori_loop(0, m - 1, greet_space, 0)
     for load in loads:
         load.wait()
 
@@ -85,34 +85,39 @@
             src_ref=src, dst_ref=dst, send_sem=send, recv_sem=recv,
             device_id=where, device_id_type=MESH)
 
+    inv_stop = [
+        jnp.exp(jnp.full((1, 1), species_bin[k].astype(jnp.float32))
+                * (-stop_span / (total_species - 1))) * (1.0 / stop_floor)
+        for k in range(local_species)]
     lanes = lax.broadcasted_iota(jnp.int32, (8, cells), 1)
 
-    for step in range(STEPS):
+    unsent = []
+
+    def run_step(step, top):
         top_send[step] = top
-        top_one[step, me] = top
+        if step == 0:
+            pl.semaphore_wait(barrier, n + m - 2)
+
+        def top_copy_one(i):
+            there = lax.rem(me + 1 + i, n)
+            return copy_to(top_send.at[step], top_one.at[step, me], top_sems.at[step, 0, i],
+                           top_sems.at[step, 1, me], (me_space, there))
+
+        def top_copy_two(i):
+            there = lax.rem(me_space + 1 + i, m)
+            return copy_to(top_mid.at[step], top_two.at[step, me_space], top_sems.at[step, 2, i],
+                           top_sems.at[step, 3, me_space], (there, me))
+
+        def start_one(i, carry):
+            top_copy_one(i).start()
+            return carry
+
+        lax.fori_loop(0, n - 1, start_one, 0)
         for f in range(fluids):
             for side, (far, near) in enumerate(((bottom - 2, bottom - 1), (TOP + 1, TOP))):
                 halo_send[step, side, f:f + 1, :] = rho[f, far:far + 1, :]
                 halo_send[step, side, fluids + f:fluids + f + 1, :] = rho[f, near:near + 1, :]
                 halo_send[step, side, 2 * fluids + f:2 * fluids + f + 1, :] = azi[f, near:near + 1, :]
-        if step == 0:
-            pl.semaphore_wait(barrier, n + m - 2)
-
-        def top_copy_one(i):
-            there = lax.rem(me + 1 + i, n)
-            return copy_to(top_send.at[step], top_one.at[step, me], top_sems.at[step, 0, i],
-                           top_sems.at[step, 1, me], (me_space, there))
-
-        def top_copy_two(i):
-            there = lax.rem(me_space + 1 + i, m)
-            return copy_to(top_mid.at[step], top_two.at[step, me_space], top_sems.at[step, 2, i],
-                           top_sems.at[step, 3, me_space], (there, me))
-
-        def start_one(i, carry):
-            top_copy_one(i).start()
-            return carry
-
-        lax.fori_loop(0, n - 1, start_one, 0)
         halos = []
         for side, there in enumerate((lax.rem(me_space + 1, m), lax.rem(me_space + m - 1, m))):
             halos.append(copy_to(halo_send.at[step, side], halo_recv.at[step, side],
@@ -121,33 +126,29 @@
         for halo in halos:
             halo.start()
 
-        def radial(i, carry):
-            f = i // groups
-            r = lax.rem(i, groups)
-            rows = pl.ds(pl.multiple_of(TOP + 8 * r, 8), 8)
-            here = rho[f, rows, :]
-            speed = rad[f, rows, :]
-            back = jnp.where(lanes >= 1, pltpu.roll(here, 1, 1), 0.0)
-            ahead = jnp.where(lanes < cells - 1, pltpu.roll(here, cells - 1, 1), 0.0)
-            down = 3.0 * here - ahead
-            down_next = jnp.where(lanes < cells - 1, pltpu.roll(down, cells - 1, 1), 0.0)
-            face = speed + jnp.where(lanes < cells - 1, pltpu.roll(speed, cells - 1, 1), 0.0)
-            flux = face * jnp.where(face > 0.0, 3.0 * here - back, down_next)
-            before = jnp.where(lanes >= 1, pltpu.roll(flux, 1, 1), jnp.minimum(speed, 0.0) * down)
-            div[f, pl.ds(pl.multiple_of(8 * r, 8), 8), :] = flux - before
-            return carry
-
-        lax.fori_loop(0, fluids * groups, radial, 0)
-
-        def gas_push(r, carry):
-            rows = pl.ds(pl.multiple_of(TOP + 8 * r, 8), 8)
-            here = rho[gas_at, rows, :]
+        def radial(f, carry):
+            for r in range(groups):
+                here = rho[f, TOP + 8 * r:TOP + 8 * r + 8, :]
+                speed = rad[f, TOP + 8 * r:TOP + 8 * r + 8, :]
+                back = jnp.where(lanes >= 1, pltpu.roll(here, 1, 1), 0.0)
+                ahead = jnp.where(lanes < cells - 1, pltpu.roll(here, cells - 1, 1), 0.0)
+                down = 3.0 * here - ahead
+                down_next = jnp.where(lanes < cells - 1, pltpu.roll(down, cells - 1, 1), 0.0)
+                face = speed + jnp.where(
+                    lanes < cells - 1, pltpu.roll(speed, cells - 1, 1), 0.0)
+                flux = face * jnp.where(face > 0.0, 3.0 * here - back, down_next)
+                before = jnp.where(
+                    lanes >= 1, pltpu.roll(flux, 1, 1), jnp.minimum(speed, 0.0) * down)
+                div[f, 8 * r:8 * r + 8, :] = flux - before
+            return carry
+
+        lax.fori_loop(0, fluids, radial, 0)
+
+        for r in range(groups):
+            here = rho[gas_at, TOP + 8 * r:TOP + 8 * r + 8, :]
             up = jnp.where(lanes < cells - 1, pltpu.roll(here, cells - 1, 1), here)
             low = jnp.where(lanes >= 1, pltpu.roll(here, 1, 1), here)
-            push[0, pl.ds(pl.multiple_of(8 * r, 8), 8), :] = (up - low) * (0.5 / here)
-            return carry
-
-        lax.fori_loop(0, groups, gas_push, 0)
+            push[0, 8 * r:8 * r + 8, :] = (up - low) * (0.5 / here)
 
         def wait_one(i, best):
             there = lax.rem(me + 1 + i, n)
@@ -245,38 +246,42 @@
                            rs_sems.at[step, 0, z], rs_sems.at[step, 1, z],
                            (me_space, 2 * z + core))
 
-        def for_sibling(i, carry):
-            z = lax.rem(chip + 1 + i, chips)
+        def farther(i):
+            return lax.rem(chip + 1 + lax.rem(chips // 2 - 1 + i, chips - 1), chips)
+
+        def for_sibling(z):
             sums = drag(2 * z + 1 - core)
             for part in range(3):
                 terms[step, 1 - core, z, part] = sums[part]
             sib_copy(z).start()
-            return carry
-
-        lax.fori_loop(0, chips, for_sibling, 0)
+
+        def for_sibling_step(i, carry):
+            for_sibling(farther(i))
+            return carry
+
+        lax.fori_loop(0, chips - 1, for_sibling_step, 0)
+        for_sibling(chip)
 
         def for_peers(i, carry):
-            z = lax.rem(chip + 1 + i, chips)
+            z = farther(i)
             sums = drag(2 * z + core)
             sib_copy(z).wait_recv()
             for part in range(3):
                 terms[step, core, z, part] = sums[part] + sib_recv[step, z, part]
-
-            @pl.when(i < chips - 1)
-            def _():
-                rs_copy(z).start()
-
-            return carry
-
-        lax.fori_loop(0, chips, for_peers, 0)
+            rs_copy(z).start()
+            return carry
+
+        lax.fori_loop(0, chips - 1, for_peers, 0)
+        sums = drag(me)
+        sib_copy(chip).wait_recv()
+        sums = tuple(sums[part] + sib_recv[step, chip, part] for part in range(3))
 
         def gather_sums(i, sums):
             z = lax.rem(chip + 1 + i, chips)
             rs_arrival(z).wait_recv()
             return tuple(sums[part] + rs_recv[step, z, part] for part in range(3))
 
-        sums = lax.fori_loop(
-            0, chips - 1, gather_sums, tuple(terms[step, core, chip, part] for part in range(3)))
+        sums = lax.fori_loop(0, chips - 1, gather_sums, sums)
 
         rows, inner, cols = place(me)
         inverse = 1.0 / (1.0 + sums[0])
@@ -302,7 +307,7 @@
                            fw_sems.at[step, 0, z], fw_sems.at[step, 1, z], (me_space, sibling))
 
         def start_ag(i, carry):
-            ag_copy(lax.rem(chip + 1 + i, chips)).start()
+            ag_copy(farther(i)).start()
             return carry
 
         lax.fori_loop(0, chips - 1, start_ag, 0)
@@ -314,6 +319,8 @@
             gas_azi = gnew[step, chunk, 1]
             rad[gas_at, rows, cols] = gas_rad
             azi[gas_at, rows, cols] = gas_azi
+            if step == STEPS - 1:
+                return best
             speed = jnp.abs(gas_rad) + jnp.abs(gas_azi)
             for k in range(local_species):
                 factor = damp[k, inner, cols]
@@ -341,6 +348,14 @@
 
         top = lax.fori_loop(0, chips, update_sibling, top)
 
+        unsent.append((top_copy_one, top_copy_two, sib_copy, rs_copy, ag_copy, fw_copy, halos))
+        return top
+
+    for step in range(STEPS):
+        top = run_step(step, top)
+
+    for top_copy_one, top_copy_two, sib_copy, rs_copy, ag_copy, fw_copy, halos in unsent:
+
         def sent_one(i, carry):
             top_copy_one(i).wait_send()
             return carry
@@ -367,16 +382,32 @@
         for halo in halos:
             halo.wait_send()
 
-    stores = []
+
+def finish(rho, rad, azi, damp, dust_out, gas_out, new, sems):
+    local_species, tile_rows, _ = damp.shape
+    interior = pl.ds(TOP, tile_rows)
+    copies = [pltpu.make_async_copy(
+        rho.at[pl.ds(0, local_species), interior], dust_out.at[0], sems.at[0])]
     for part, held in enumerate((rho, rad, azi)):
-        stores.append(pltpu.make_async_copy(
-            held.at[pl.ds(0, local_species), interior], dust_out.at[part], io_sem.at[2 * part]))
-        stores.append(pltpu.make_async_copy(
-            held.at[gas_at, interior], gas_out.at[part], io_sem.at[2 * part + 1]))
-    for store in stores:
-        store.start()
-    for store in stores:
-        store.wait()
+        copies.append(pltpu.make_async_copy(
+            held.at[local_species, interior], gas_out.at[part], sems.at[1 + part]))
+    for copy in copies:
+        copy.start()
+    for k in range(local_species):
+        for r in range(tile_rows // 8):
+            rows = slice(TOP + 8 * r, TOP + 8 * r + 8)
+            inner = slice(8 * r, 8 * r + 8)
+            factor = damp[k, inner, :]
+            for part, held in enumerate((rad, azi)):
+                gas = held[local_species, rows, :]
+                new[part, k, inner, :] = gas + (held[k, rows, :] - gas) * factor
+        for part in range(2):
+            copy = pltpu.make_async_copy(
+                new.at[part, k], dust_out.at[part + 1, k], sems.at[4 + 2 * k + part])
+            copy.start()
+            copies.append(copy)
+    for copy in copies:
+        copy.wait()
 
 
 def solution(mesh):
@@ -389,26 +420,22 @@
         groups = tile_rows // 8
         width = cells // (n // groups)
         chips = n // 2
-        total_species = local_species * n
-        inv_stop = jnp.exp(
-            -stop_span * species_bin.astype(jnp.float32) / (total_species - 1)
-        ) / stop_floor
         f32 = jnp.float32
         halo_rows = -(-3 * fluids // 8) * 8
         extended = pltpu.VMEM((fluids, tile_rows + 16, cells), f32)
+        damped = pltpu.VMEM((local_species, tile_rows, cells), f32)
         dma = pltpu.SemaphoreType.DMA
-        return pl.pallas_call(
+        near = pl.BlockSpec(memory_space=pltpu.VMEM)
+        far = pl.BlockSpec(memory_space=pltpu.HBM)
+        held = pl.pallas_call(
             functools.partial(kernel, n, m),
-            out_shape=(jax.ShapeDtypeStruct(dust_state.shape, f32),
-                       jax.ShapeDtypeStruct(gas_state.shape, f32)),
-            in_specs=[pl.BlockSpec(memory_space=pl.ANY), pl.BlockSpec(memory_space=pl.ANY),
-                      pl.BlockSpec(memory_space=pltpu.SMEM)],
-            out_specs=(pl.BlockSpec(memory_space=pl.ANY), pl.BlockSpec(memory_space=pl.ANY)),
+            out_shape=(extended, extended, extended, damped),
+            in_specs=[far, far, far],
+            out_specs=(near,) * 4,
             scratch_shapes=[
-                extended, extended, extended,
+                pltpu.SMEM((local_species,), jnp.int32),
                 pltpu.VMEM((fluids, tile_rows, cells), f32),
                 pltpu.VMEM((2, tile_rows, cells), f32),
-                pltpu.VMEM((local_species, tile_rows, cells), f32),
                 pltpu.VMEM((STEPS, 2, chips, 3, 8, width), f32),
                 pltpu.VMEM((STEPS, n, 2, 8, width), f32),
                 pltpu.VMEM((STEPS, chips, 3, 8, width), f32),
@@ -419,7 +446,7 @@
                 pltpu.VMEM((STEPS, m, 8, 128), f32),
                 pltpu.VMEM((STEPS, 2, halo_rows, cells), f32),
                 pltpu.VMEM((STEPS, 2, halo_rows, cells), f32),
-                dma((6,)),
+                dma((7,)),
                 dma((STEPS, 4, max(n, m))),
                 dma((STEPS, 2, 2)),
                 dma((STEPS, 2, chips)),
@@ -428,12 +455,25 @@
                 dma((STEPS, 2, chips)),
             ],
             compiler_params=pltpu.CompilerParams(
-                collective_id=0, has_side_effects=True, vmem_limit_bytes=56 * 1024 * 1024),
+                collective_id=0, has_side_effects=True, vmem_limit_bytes=58 * 1024 * 1024),
             cost_estimate=pl.CostEstimate(
                 flops=200 * fluids * tile_rows * cells,
                 bytes_accessed=24 * fluids * tile_rows * cells, transcendentals=0),
             name="disk_steps",
-        )(dust_state, gas_state, inv_stop)
+        )(dust_state, gas_state, species_bin)
+        return pl.pallas_call(
+            finish,
+            out_shape=(jax.ShapeDtypeStruct(dust_state.shape, f32),
+                       jax.ShapeDtypeStruct(gas_state.shape, f32)),
+            in_specs=[near] * 4,
+            out_specs=(far, far),
+            scratch_shapes=[
+                pltpu.VMEM((2, local_species, tile_rows, cells), f32),
+                dma((4 + 2 * local_species,)),
+            ],
+            compiler_params=pltpu.CompilerParams(vmem_limit_bytes=20 * 1024 * 1024),
+            name="last_update",
+        )(*held)
 
     return jax.shard_map(
         local,

time: 54.9 us -> 47.6 us (0.87)
  local copies, waits for them, and re-layouts: 3.53 us -> 0 us
  Pallas kernels: 49.3 us -> 46.7 us
  other arithmetic: 1.18 us -> 0 us
    unnamed x4 -> x0, local copies, waits for them, and re-layouts: 3.53 us -> none
    pallas_call x1 -> x2, Pallas kernels: 49.3 us -> 46.7 us  [the longest x1 45.3 us: local(): pl.pallas_call(functools.partial(kernel, n, m), out_shape=(extended, exte...]
    div x1 -> x0, other arithmetic: 1.18 us -> none  [local(): jnp.exp(-stop_span * species_bin.astype(jnp.float32) / (total_species - 1))]
where the time goes in v2:
time: 47.6 us; the launch traced here: 47.3 us
  Pallas kernels  46.7 us (98%)
  between operations  0.64 us (1%)
    pallas_call x1, Pallas kernels, local(): pl.pallas_call(functools.partial(kernel, n, m), out_shape=(extended, exte...  45.3 us
    pallas_call x1, Pallas kernels, local(): pl.pallas_call(finish, out_shape=(jax.ShapeDtypeStruct(dust_state.shape,...  1.36 us

profile of v2, /device:TPU:0, one launch (start us, length us, event | category | flops | bytes accessed | tf_op | source)
XLA Modules:
  0.0 47.3 jit_solution(6985621384917749357)
XLA Ops:
  0.6 45.3 %disk_steps.1 = (f32[5,48,1024]{2,1,0:T(8,128)S(1)}, f32[5,48,1024]{2,1,0:T(8,128)S(1)}, f32[5,48,1024]{2,1,0:T(8,128)S(1)}, f32[4,32,1024]{2,1,0:T(8,128)S(1)}) custom-call(f32[3,4,32,1024]{3,2,1,0:T(8,128)} %dust.1, f32[3,32,1024]{2,1,0:T(8,128)} %gas.1, s32[4]{0:T(128)} %species_bins.1), custom_call_target="tpu_custom_call" | custom-call | flops 32768000 | bytes 3932160 | tf_op jit(solution)/shard_map/disk_steps/pallas_call | solution.py:430
  46.0 1.4 %last_update.1 = (f32[3,4,32,1024]{3,2,1,0:T(8,128)}, f32[3,32,1024]{2,1,0:T(8,128)}) custom-call(f32[5,48,1024]{2,1,0:T(8,128)S(1)} %get-tuple-element.6.rho, f32[5,48,1024]{2,1,0:T(8,128)S(1)} %get-tuple-element.7.rad, f32[5,48,1024]{2,1,0:T(8,128)S(1)} %get-tuple-element.8.azi, f32[4,32,1024]{2,1,0:T(8,128)S(1)} %get-tuple-element.9.damp), custom_call_target="tpu_custom_call" | custom-call | tf_op jit(solution)/shard_map/last_update/pallas_call | solution.py:464

commit v3 on v2

--- a/solution.py
+++ b/solution.py
@@ -16,12 +16,13 @@
 
 MESH = pl.DeviceIdType.MESH
 TOP = 8
+HALVES = 2
 
 
 def kernel(
     n, m, dust, gas, species_bins, rho, rad, azi, damp,
     species_bin, div, push, terms, gnew,
-    sib_recv, rs_recv, top_send, top_one, top_mid, top_two, halo_send, halo_recv,
+    sib_recv, rs_recv, top_send, top_one, top_mid, top_two, rho_send, rho_recv, azi_send, azi_recv,
     io_sem, top_sems, halo_sems, sib_sems, rs_sems, ag_sems, fw_sems,
 ):
     local_species, tile_rows, cells = dust.shape[1:]
@@ -30,6 +31,8 @@
     groups = tile_rows // 8
     spans = n // groups
     width = cells // spans
+    halves = min(HALVES, width // 128)
+    span = width // halves
     chips = n // 2
     total_species = local_species * n
     bottom = TOP + tile_rows
@@ -91,6 +94,35 @@
         for k in range(local_species)]
     lanes = lax.broadcasted_iota(jnp.int32, (8, cells), 1)
 
+    neighbours = (lax.rem(me_space + 1, m), lax.rem(me_space + m - 1, m))
+    edges = ((bottom - 2, bottom - 1), (TOP + 1, TOP))
+    beyond = ((TOP - 2, TOP - 1), (bottom + 1, bottom))
+
+    def rho_halos(step):
+        return [copy_to(rho_send.at[step, side], rho_recv.at[step, side],
+                        halo_sems.at[step, 0, side], halo_sems.at[step, 1, side], (there, me))
+                for side, there in enumerate(neighbours)]
+
+    def azi_halos(step):
+        return [copy_to(azi_send.at[step, side], azi_recv.at[step, side],
+                        halo_sems.at[step, 2, side], halo_sems.at[step, 3, side], (there, me))
+                for side, there in enumerate(neighbours)]
+
+    def send_rho(step):
+        for side, (far, near) in enumerate(edges):
+            for f in range(fluids):
+                rho_send[step, side, f:f + 1, :] = rho[f, far:far + 1, :]
+                rho_send[step, side, fluids + f:fluids + f + 1, :] = rho[f, near:near + 1, :]
+        for halo in rho_halos(step):
+            halo.start()
+
+    def send_azi(step):
+        for side, (_, near) in enumerate(edges):
+            for f in range(fluids):
+                azi_send[step, side, f:f + 1, :] = azi[f, near:near + 1, :]
+        for halo in azi_halos(step):
+            halo.start()
+
     unsent = []
 
     def run_step(step, top):
@@ -99,32 +131,23 @@
             pl.semaphore_wait(barrier, n + m - 2)
 
         def top_copy_one(i):
+            there = lax.rem(me_space + 1 + i, m)
+            return copy_to(top_send.at[step], top_one.at[step, me_space], top_sems.at[step, 0, i],
+                           top_sems.at[step, 1, me_space], (there, me))
+
+        def top_copy_two(i):
             there = lax.rem(me + 1 + i, n)
-            return copy_to(top_send.at[step], top_one.at[step, me], top_sems.at[step, 0, i],
-                           top_sems.at[step, 1, me], (me_space, there))
-
-        def top_copy_two(i):
-            there = lax.rem(me_space + 1 + i, m)
-            return copy_to(top_mid.at[step], top_two.at[step, me_space], top_sems.at[step, 2, i],
-                           top_sems.at[step, 3, me_space], (there, me))
+            return copy_to(top_mid.at[step], top_two.at[step, me], top_sems.at[step, 2, i],
+                           top_sems.at[step, 3, me], (me_space, there))
 
         def start_one(i, carry):
             top_copy_one(i).start()
             return carry
 
-        lax.fori_loop(0, n - 1, start_one, 0)
-        for f in range(fluids):
-            for side, (far, near) in enumerate(((bottom - 2, bottom - 1), (TOP + 1, TOP))):
-                halo_send[step, side, f:f + 1, :] = rho[f, far:far + 1, :]
-                halo_send[step, side, fluids + f:fluids + f + 1, :] = rho[f, near:near + 1, :]
-                halo_send[step, side, 2 * fluids + f:2 * fluids + f + 1, :] = azi[f, near:near + 1, :]
-        halos = []
-        for side, there in enumerate((lax.rem(me_space + 1, m), lax.rem(me_space + m - 1, m))):
-            halos.append(copy_to(halo_send.at[step, side], halo_recv.at[step, side],
-                                 halo_sems.at[step, 0, side], halo_sems.at[step, 1, side],
-                                 (there, me)))
-        for halo in halos:
-            halo.start()
+        lax.fori_loop(0, m - 1, start_one, 0)
+        send_azi(step)
+        if step == 0:
+            send_rho(step)
 
         def radial(f, carry):
             for r in range(groups):
@@ -151,28 +174,27 @@
             push[0, 8 * r:8 * r + 8, :] = (up - low) * (0.5 / here)
 
         def wait_one(i, best):
-            there = lax.rem(me + 1 + i, n)
+            there = lax.rem(me_space + 1 + i, m)
             copy_to(top_send.at[step], top_one.at[step, there], top_sems.at[step, 0, i],
-                    top_sems.at[step, 1, there], (me_space, there)).wait_recv()
+                    top_sems.at[step, 1, there], (there, me)).wait_recv()
             return jnp.maximum(best, top_one[step, there])
 
-        top = lax.fori_loop(0, n - 1, wait_one, top)
+        top = lax.fori_loop(0, m - 1, wait_one, top)
         top_mid[step] = top
 
         def start_two(i, carry):
             top_copy_two(i).start()
             return carry
 
-        lax.fori_loop(0, m - 1, start_two, 0)
-
-        for halo in halos:
+        lax.fori_loop(0, n - 1, start_two, 0)
+
+        for halo in azi_halos(step) + rho_halos(step):
             halo.wait_recv()
-        for f in range(fluids):
-            for side, (far, near) in enumerate(((TOP - 2, TOP - 1), (bottom + 1, bottom))):
-                rho[f, far:far + 1, :] = halo_recv[step, side, f:f + 1, :]
-                rho[f, near:near + 1, :] = halo_recv[step, side, fluids + f:fluids + f + 1, :]
-                azi[f, near:near + 1, :] = halo_recv[
-                    step, side, 2 * fluids + f:2 * fluids + f + 1, :]
+        for side, (far, near) in enumerate(beyond):
+            for f in range(fluids):
+                rho[f, far:far + 1, :] = rho_recv[step, side, f:f + 1, :]
+                rho[f, near:near + 1, :] = rho_recv[step, side, fluids + f:fluids + f + 1, :]
+                azi[f, near:near + 1, :] = azi_recv[step, side, f:f + 1, :]
 
         def azimuthal(f, carry):
             for r in range(groups):
@@ -198,28 +220,28 @@
             ) * (0.5 / rho[gas_at, at:at + 8, :])
 
         def wait_two(i, best):
-            there = lax.rem(me_space + 1 + i, m)
+            there = lax.rem(me + 1 + i, n)
             copy_to(top_mid.at[step], top_two.at[step, there], top_sems.at[step, 2, i],
-                    top_sems.at[step, 3, there], (there, me)).wait_recv()
+                    top_sems.at[step, 3, there], (me_space, there)).wait_recv()
             return jnp.maximum(best, top_two[step, there])
 
-        top = lax.fori_loop(0, m - 1, wait_two, top)
+        top = lax.fori_loop(0, n - 1, wait_two, top)
         fastest = jnp.max(jnp.max(top, axis=0, keepdims=True), axis=1, keepdims=True)
         dt = courant / (sound_speed + fastest)
         dt_quarter = 0.25 * dt
 
-        def place(chunk):
+        def place(chunk, h):
             r = chunk // spans
-            g = lax.rem(chunk, spans)
-            cols = pl.ds(pl.multiple_of(width * g, 128), width)
+            start = width * lax.rem(chunk, spans) + span * h
             return (pl.ds(pl.multiple_of(TOP + 8 * r, 8), 8),
-                    pl.ds(pl.multiple_of(8 * r, 8), 8), cols)
-
-        def drag(chunk):
-            rows, inner, cols = place(chunk)
+                    pl.ds(pl.multiple_of(8 * r, 8), 8),
+                    pl.ds(pl.multiple_of(start, 128), span))
+
+        def drag(chunk, h):
+            rows, inner, cols = place(chunk, h)
             new_gas = rho[gas_at, rows, cols] - dt_quarter * div[gas_at, inner, cols]
             rho[gas_at, rows, cols] = new_gas
-            sums = [jnp.zeros((8, width), jnp.float32)] * 3
+            sums = [jnp.zeros((8, span), jnp.float32)] * 3
             for k in range(local_species):
                 scale = dt * inv_stop[k]
                 new = rho[k, rows, cols] - dt_quarter * div[k, inner, cols]
@@ -232,91 +254,105 @@
                 sums[2] = sums[2] + weight * azi[k, rows, cols]
             return sums
 
-        def sib_copy(i):
-            return copy_to(terms.at[step, 1 - core, i], sib_recv.at[step, i],
-                           sib_sems.at[step, 0, i], sib_sems.at[step, 1, i], (me_space, sibling))
-
-        def rs_copy(z):
-            return copy_to(terms.at[step, core, z], rs_recv.at[step, chip],
-                           rs_sems.at[step, 0, z], rs_sems.at[step, 1, chip],
-                           (me_space, 2 * z + core))
-
-        def rs_arrival(z):
-            return copy_to(terms.at[step, core, z], rs_recv.at[step, z],
-                           rs_sems.at[step, 0, z], rs_sems.at[step, 1, z],
-                           (me_space, 2 * z + core))
-
         def farther(i):
             return lax.rem(chip + 1 + lax.rem(chips // 2 - 1 + i, chips - 1), chips)
 
-        def for_sibling(z):
-            sums = drag(2 * z + 1 - core)
-            for part in range(3):
-                terms[step, 1 - core, z, part] = sums[part]
-            sib_copy(z).start()
-
-        def for_sibling_step(i, carry):
-            for_sibling(farther(i))
-            return carry
-
-        lax.fori_loop(0, chips - 1, for_sibling_step, 0)
-        for_sibling(chip)
-
-        def for_peers(i, carry):
-            z = farther(i)
-            sums = drag(2 * z + core)
-            sib_copy(z).wait_recv()
-            for part in range(3):
-                terms[step, core, z, part] = sums[part] + sib_recv[step, z, part]
-            rs_copy(z).start()
-            return carry
-
-        lax.fori_loop(0, chips - 1, for_peers, 0)
-        sums = drag(me)
-        sib_copy(chip).wait_recv()
-        sums = tuple(sums[part] + sib_recv[step, chip, part] for part in range(3))
-
-        def gather_sums(i, sums):
-            z = lax.rem(chip + 1 + i, chips)
-            rs_arrival(z).wait_recv()
-            return tuple(sums[part] + rs_recv[step, z, part] for part in range(3))
-
-        sums = lax.fori_loop(0, chips - 1, gather_sums, sums)
-
-        rows, inner, cols = place(me)
-        inverse = 1.0 / (1.0 + sums[0])
-        gnew[step, me, 0] = (rad[gas_at, rows, cols] - dt * push[0, inner, cols] + sums[1]) * inverse
-        gnew[step, me, 1] = (azi[gas_at, rows, cols] - dt * push[1, inner, cols] + sums[2]) * inverse
-
-        def ag_copy(z):
-            return copy_to(gnew.at[step, me], gnew.at[step, me], ag_sems.at[step, 0, z],
-                           ag_sems.at[step, 1, chip], (me_space, 2 * z + core))
-
-        def ag_arrival(z):
-            return copy_to(gnew.at[step, 2 * z + core], gnew.at[step, 2 * z + core],
-                           ag_sems.at[step, 0, z], ag_sems.at[step, 1, z],
+        def sib_copy(z, h):
+            return copy_to(terms.at[step, 1 - core, z, h], sib_recv.at[step, z, h],
+                           sib_sems.at[step, 0, z, h], sib_sems.at[step, 1, z, h],
+                           (me_space, sibling))
+
+        def rs_copy(z, h):
+            return copy_to(terms.at[step, core, z, h], rs_recv.at[step, chip, h],
+                           rs_sems.at[step, 0, z, h], rs_sems.at[step, 1, chip, h],
                            (me_space, 2 * z + core))
 
-        def fw_copy(z):
-            return copy_to(gnew.at[step, 2 * z + core], gnew.at[step, 2 * z + core],
-                           fw_sems.at[step, 0, z], fw_sems.at[step, 1, z], (me_space, sibling))
-
-        def fw_arrival(z):
-            other = 2 * z + 1 - core
-            return copy_to(gnew.at[step, other], gnew.at[step, other],
-                           fw_sems.at[step, 0, z], fw_sems.at[step, 1, z], (me_space, sibling))
-
-        def start_ag(i, carry):
-            ag_copy(farther(i)).start()
-            return carry
-
-        lax.fori_loop(0, chips - 1, start_ag, 0)
-        fw_copy(chip).start()
-
-        def update(chunk, best):
-            rows, inner, cols = place(chunk)
-            gas_rad = gnew[step, chunk, 0]
-            gas_azi = gnew[step, chunk, 1]
+        def rs_arrival(z, h):
+            return copy_to(terms.at[step, core, z, h], rs_recv.at[step, z, h],
+                           rs_sems.at[step, 0, z, h], rs_sems.at[step, 1, z, h],
+                           (me_space, 2 * z + core))
+
+        def ag_copy(z, h):
+            return copy_to(gnew.at[step, me, h], gnew.at[step, me, h], ag_sems.at[step, 0, z, h],
+                           ag_sems.at[step, 1, chip, h], (me_space, 2 * z + core))
+
+        def ag_arrival(z, h):
+            there = 2 * z + core
+            return copy_to(gnew.at[step, there, h], gnew.at[step, there, h],
+                           ag_sems.at[step, 0, z, h], ag_sems.at[step, 1, z, h],
+                           (me_space, there))
+
+        def fw_copy(z, h):
+            there = 2 * z + core
+            return copy_to(gnew.at[step, there, h], gnew.at[step, there, h],
+                           fw_sems.at[step, 0, z, h], fw_sems.at[step, 1, z, h],
+                           (me_space, sibling))
+
+        def fw_arrival(z, h):
+            there = 2 * z + 1 - core
+            return copy_to(gnew.at[step, there, h], gnew.at[step, there, h],
+                           fw_sems.at[step, 0, z, h], fw_sems.at[step, 1, z, h],
+                           (me_space, sibling))
+
+        own = []
+        for h in range(halves):
+            def for_sibling(z):
+                sums = drag(2 * z + 1 - core, h)
+                for part in range(3):
+                    terms[step, 1 - core, z, h, part] = sums[part]
+                sib_copy(z, h).start()
+
+            def for_sibling_step(i, carry):
+                for_sibling(farther(i))
+                return carry
+
+            lax.fori_loop(0, chips - 1, for_sibling_step, 0)
+            for_sibling(chip)
+
+            def for_peers(i, carry):
+                z = farther(i)
+                sums = drag(2 * z + core, h)
+                sib_copy(z, h).wait_recv()
+                for part in range(3):
+                    terms[step, core, z, h, part] = sums[part] + sib_recv[step, z, h, part]
+                rs_copy(z, h).start()
+                return carry
+
+            lax.fori_loop(0, chips - 1, for_peers, 0)
+            own.append(drag(me, h))
+
+        if step + 1 < STEPS:
+            send_rho(step + 1)
+
+        for h in range(halves):
+            sib_copy(chip, h).wait_recv()
+
+            def gather_sums(i, sums):
+                z = lax.rem(chip + 1 + i, chips)
+                rs_arrival(z, h).wait_recv()
+                return tuple(sums[part] + rs_recv[step, z, h, part] for part in range(3))
+
+            sums = lax.fori_loop(
+                0, chips - 1, gather_sums,
+                tuple(own[h][part] + sib_recv[step, chip, h, part] for part in range(3)))
+            rows, inner, cols = place(me, h)
+            inverse = 1.0 / (1.0 + sums[0])
+            gnew[step, me, h, 0] = (
+                rad[gas_at, rows, cols] - dt * push[0, inner, cols] + sums[1]) * inverse
+            gnew[step, me, h, 1] = (
+                azi[gas_at, rows, cols] - dt * push[1, inner, cols] + sums[2]) * inverse
+
+            def start_ag(i, carry):
+                ag_copy(farther(i), h).start()
+                return carry
+
+            lax.fori_loop(0, chips - 1, start_ag, 0)
+            fw_copy(chip, h).start()
+
+        def update(chunk, h, best):
+            rows, inner, cols = place(chunk, h)
+            gas_rad = gnew[step, chunk, h, 0]
+            gas_azi = gnew[step, chunk, h, 1]
             rad[gas_at, rows, cols] = gas_rad
             azi[gas_at, rows, cols] = gas_azi
             if step == STEPS - 1:
@@ -331,24 +367,27 @@
                 speed = jnp.maximum(speed, jnp.abs(new_rad) + jnp.abs(new_azi))
             return jnp.maximum(best, fold(speed))
 
-        top = update(me, jnp.zeros((8, 128), jnp.float32))
-
-        def update_peer(i, best):
-            z = lax.rem(chip + 1 + i, chips)
-            ag_arrival(z).wait_recv()
-            fw_copy(z).start()
-            return update(2 * z + core, best)
-
-        top = lax.fori_loop(0, chips - 1, update_peer, top)
-
-        def update_sibling(i, best):
-            z = lax.rem(chip + i, chips)
-            fw_arrival(z).wait_recv()
-            return update(2 * z + 1 - core, best)
-
-        top = lax.fori_loop(0, chips, update_sibling, top)
-
-        unsent.append((top_copy_one, top_copy_two, sib_copy, rs_copy, ag_copy, fw_copy, halos))
+        top = jnp.zeros((8, 128), jnp.float32)
+        for h in range(halves):
+            top = update(me, h, top)
+
+            def update_peer(i, best):
+                z = lax.rem(chip + 1 + i, chips)
+                ag_arrival(z, h).wait_recv()
+                fw_copy(z, h).start()
+                return update(2 * z + core, h, best)
+
+            top = lax.fori_loop(0, chips - 1, update_peer, top)
+
+            def update_sibling(i, best):
+                z = lax.rem(chip + i, chips)
+                fw_arrival(z, h).wait_recv()
+                return update(2 * z + 1 - core, h, best)
+
+            top = lax.fori_loop(0, chips, update_sibling, top)
+
+        unsent.append((top_copy_one, top_copy_two, sib_copy, rs_copy, ag_copy, fw_copy,
+                       rho_halos(step) + azi_halos(step)))
         return top
 
     for step in range(STEPS):
@@ -365,18 +404,20 @@
             return carry
 
         def sent_core(i, carry):
-            sib_copy(i).wait_send()
-            fw_copy(i).wait_send()
+            for h in range(halves):
+                sib_copy(i, h).wait_send()
+                fw_copy(i, h).wait_send()
             return carry
 
         def sent_chip(i, carry):
             z = lax.rem(chip + 1 + i, chips)
-            rs_copy(z).wait_send()
-            ag_copy(z).wait_send()
-            return carry
-
-        lax.fori_loop(0, n - 1, sent_one, 0)
-        lax.fori_loop(0, m - 1, sent_two, 0)
+            for h in range(halves):
+                rs_copy(z, h).wait_send()
+                ag_copy(z, h).wait_send()
+            return carry
+
+        lax.fori_loop(0, m - 1, sent_one, 0)
+        lax.fori_loop(0, n - 1, sent_two, 0)
         lax.fori_loop(0, chips, sent_core, 0)
         lax.fori_loop(0, chips - 1, sent_chip, 0)
         for halo in halos:
@@ -419,9 +460,12 @@
         fluids = local_species + 1
         groups = tile_rows // 8
         width = cells // (n // groups)
+        halves = min(HALVES, width // 128)
+        span = width // halves
         chips = n // 2
         f32 = jnp.float32
-        halo_rows = -(-3 * fluids // 8) * 8
+        rho_rows = -(-2 * fluids // 8) * 8
+        azi_rows = -(-fluids // 8) * 8
         extended = pltpu.VMEM((fluids, tile_rows + 16, cells), f32)
         damped = pltpu.VMEM((local_species, tile_rows, cells), f32)
         dma = pltpu.SemaphoreType.DMA
@@ -436,23 +480,25 @@
                 pltpu.SMEM((local_species,), jnp.int32),
                 pltpu.VMEM((fluids, tile_rows, cells), f32),
                 pltpu.VMEM((2, tile_rows, cells), f32),
-                pltpu.VMEM((STEPS, 2, chips, 3, 8, width), f32),
-                pltpu.VMEM((STEPS, n, 2, 8, width), f32),
-                pltpu.VMEM((STEPS, chips, 3, 8, width), f32),
-                pltpu.VMEM((STEPS, chips, 3, 8, width), f32),
+                pltpu.VMEM((STEPS, 2, chips, halves, 3, 8, span), f32),
+                pltpu.VMEM((STEPS, n, halves, 2, 8, span), f32),
+                pltpu.VMEM((STEPS, chips, halves, 3, 8, span), f32),
+                pltpu.VMEM((STEPS, chips, halves, 3, 8, span), f32),
+                pltpu.VMEM((STEPS, 8, 128), f32),
+                pltpu.VMEM((STEPS, m, 8, 128), f32),
                 pltpu.VMEM((STEPS, 8, 128), f32),
                 pltpu.VMEM((STEPS, n, 8, 128), f32),
-                pltpu.VMEM((STEPS, 8, 128), f32),
-                pltpu.VMEM((STEPS, m, 8, 128), f32),
-                pltpu.VMEM((STEPS, 2, halo_rows, cells), f32),
-                pltpu.VMEM((STEPS, 2, halo_rows, cells), f32),
+                pltpu.VMEM((STEPS, 2, rho_rows, cells), f32),
+                pltpu.VMEM((STEPS, 2, rho_rows, cells), f32),
+                pltpu.VMEM((STEPS, 2, azi_rows, cells), f32),
+                pltpu.VMEM((STEPS, 2, azi_rows, cells), f32),
                 dma((7,)),
                 dma((STEPS, 4, max(n, m))),
-                dma((STEPS, 2, 2)),
-                dma((STEPS, 2, chips)),
-                dma((STEPS, 2, chips)),
-                dma((STEPS, 2, chips)),
-                dma((STEPS, 2, chips)),
+                dma((STEPS, 4, 2)),
+                dma((STEPS, 2, chips, halves)),
+                dma((STEPS, 2, chips, halves)),
+                dma((STEPS, 2, chips, halves)),
+                dma((STEPS, 2, chips, halves)),
             ],
             compiler_params=pltpu.CompilerParams(
                 collective_id=0, has_side_effects=True, vmem_limit_bytes=58 * 1024 * 1024),

time: 47.6 us -> 47.1 us (0.989)
  Pallas kernels: 46.7 us -> 46.1 us
    pallas_call x1, Pallas kernels: 45.3 us -> 44.8 us  [local(): pl.pallas_call(functools.partial(kernel, n, m), out_shape=(extended, exte...]
where the time goes in v3:
time: 47.1 us; the launch traced here: 46.8 us
  Pallas kernels  46.1 us (98%)
  between operations  0.64 us (1%)
    pallas_call x1, Pallas kernels, local(): pl.pallas_call(functools.partial(kernel, n, m), out_shape=(extended, exte...  44.8 us
    pallas_call x1, Pallas kernels, local(): pl.pallas_call(finish, out_shape=(jax.ShapeDtypeStruct(dust_state.shape,...  1.36 us

profile of v3, /device:TPU:0, one launch (start us, length us, event | category | flops | bytes accessed | tf_op | source)
XLA Modules:
  0.0 46.8 jit_solution(4056168128462436006)
XLA Ops:
  0.6 44.8 %disk_steps.1 = (f32[5,48,1024]{2,1,0:T(8,128)S(1)}, f32[5,48,1024]{2,1,0:T(8,128)S(1)}, f32[5,48,1024]{2,1,0:T(8,128)S(1)}, f32[4,32,1024]{2,1,0:T(8,128)S(1)}) custom-call(f32[3,4,32,1024]{3,2,1,0:T(8,128)} %dust.1, f32[3,32,1024]{2,1,0:T(8,128)} %gas.1, s32[4]{0:T(128)} %species_bins.1), custom_call_target="tpu_custom_call" | custom-call | flops 32768000 | bytes 3932160 | tf_op jit(solution)/shard_map/disk_steps/pallas_call | solution.py:474
  45.4 1.4 %last_update.1 = (f32[3,4,32,1024]{3,2,1,0:T(8,128)}, f32[3,32,1024]{2,1,0:T(8,128)}) custom-call(f32[5,48,1024]{2,1,0:T(8,128)S(1)} %get-tuple-element.6.rho, f32[5,48,1024]{2,1,0:T(8,128)S(1)} %get-tuple-element.7.rad, f32[5,48,1024]{2,1,0:T(8,128)S(1)} %get-tuple-element.8.azi, f32[4,32,1024]{2,1,0:T(8,128)S(1)} %get-tuple-element.9.damp), custom_call_target="tpu_custom_call" | custom-call | tf_op jit(solution)/shard_map/last_update/pallas_call | solution.py:510

commit v4 on v3

--- a/solution.py
+++ b/solution.py
@@ -16,7 +16,15 @@
 
 MESH = pl.DeviceIdType.MESH
 TOP = 8
-HALVES = 2
+HALVES = 1
+
+
+def loop(count, body, carry):
+    if count > 8:
+        return lax.fori_loop(0, count, body, carry)
+    for i in range(count):
+        carry = body(i, carry)
+    return carry
 
 
 def kernel(
@@ -56,8 +64,8 @@
             barrier, inc=1, device_id=(lax.rem(me_space + 1 + i, m), me), device_id_type=MESH)
         return carry
 
-    lax.fori_loop(0, n - 1, greet_species, 0)
-    lax.fori_loop(0, m - 1, greet_space, 0)
+    loop(n - 1, greet_species, 0)
+    loop(m - 1, greet_space, 0)
     loads = []
     for part, held in enumerate((rho, rad, azi)):
         loads.append(pltpu.make_async_copy(
@@ -76,12 +84,13 @@
             best = jnp.maximum(best, values[:, start:start + 128])
         return best
 
-    def first_top(i, best):
-        f = i // groups
-        rows = pl.ds(pl.multiple_of(TOP + 8 * lax.rem(i, groups), 8), 8)
-        return jnp.maximum(best, fold(jnp.abs(rad[f, rows, :]) + jnp.abs(azi[f, rows, :])))
-
-    top = lax.fori_loop(0, fluids * groups, first_top, jnp.zeros((8, 128), jnp.float32))
+    def first_top(f, best):
+        for at in range(TOP, bottom, 8):
+            best = jnp.maximum(
+                best, fold(jnp.abs(rad[f, at:at + 8, :]) + jnp.abs(azi[f, at:at + 8, :])))
+        return best
+
+    top = lax.fori_loop(0, fluids, first_top, jnp.zeros((8, 128), jnp.float32))
 
     def copy_to(src, dst, send, recv, where):
         return pltpu.make_async_remote_copy(
@@ -132,19 +141,27 @@
 
         def top_copy_one(i):
             there = lax.rem(me_space + 1 + i, m)
-            return copy_to(top_send.at[step], top_one.at[step, me_space], top_sems.at[step, 0, i],
-                           top_sems.at[step, 1, me_space], (there, me))
+            return copy_to(top_send.at[step], top_one.at[step, i], top_sems.at[step, 0],
+                           top_sems.at[step, 1], (there, me))
 
         def top_copy_two(i):
             there = lax.rem(me + 1 + i, n)
-            return copy_to(top_mid.at[step], top_two.at[step, me], top_sems.at[step, 2, i],
-                           top_sems.at[step, 3, me], (me_space, there))
+            return copy_to(top_mid.at[step], top_two.at[step, i], top_sems.at[step, 2],
+                           top_sems.at[step, 3], (me_space, there))
+
+        def top_all_one():
+            return copy_to(top_one.at[step], top_one.at[step], top_sems.at[step, 0],
+                           top_sems.at[step, 1], (neighbours[0], me))
+
+        def top_all_two():
+            return copy_to(top_two.at[step], top_two.at[step], top_sems.at[step, 2],
+                           top_sems.at[step, 3], (me_space, sibling))
 
         def start_one(i, carry):
             top_copy_one(i).start()
             return carry
 
-        lax.fori_loop(0, m - 1, start_one, 0)
+        loop(m - 1, start_one, 0)
         send_azi(step)
         if step == 0:
             send_rho(step)
@@ -173,20 +190,16 @@
             low = jnp.where(lanes >= 1, pltpu.roll(here, 1, 1), here)
             push[0, 8 * r:8 * r + 8, :] = (up - low) * (0.5 / here)
 
-        def wait_one(i, best):
-            there = lax.rem(me_space + 1 + i, m)
-            copy_to(top_send.at[step], top_one.at[step, there], top_sems.at[step, 0, i],
-                    top_sems.at[step, 1, there], (there, me)).wait_recv()
-            return jnp.maximum(best, top_one[step, there])
-
-        top = lax.fori_loop(0, m - 1, wait_one, top)
+        top_all_one().wait_recv()
+        for i in range(m - 1):
+            top = jnp.maximum(top, top_one[step, i])
         top_mid[step] = top
 
         def start_two(i, carry):
             top_copy_two(i).start()
             return carry
 
-        lax.fori_loop(0, n - 1, start_two, 0)
+        loop(n - 1, start_two, 0)
 
         for halo in azi_halos(step) + rho_halos(step):
             halo.wait_recv()
@@ -219,13 +232,9 @@
                 rho[gas_at, at + 1:at + 9, :] - rho[gas_at, at - 1:at + 7, :]
             ) * (0.5 / rho[gas_at, at:at + 8, :])
 
-        def wait_two(i, best):
-            there = lax.rem(me + 1 + i, n)
-            copy_to(top_mid.at[step], top_two.at[step, there], top_sems.at[step, 2, i],
-                    top_sems.at[step, 3, there], (me_space, there)).wait_recv()
-            return jnp.maximum(best, top_two[step, there])
-
-        top = lax.fori_loop(0, n - 1, wait_two, top)
+        top_all_two().wait_recv()
+        for i in range(n - 1):
+            top = jnp.maximum(top, top_two[step, i])
         fastest = jnp.max(jnp.max(top, axis=0, keepdims=True), axis=1, keepdims=True)
         dt = courant / (sound_speed + fastest)
         dt_quarter = 0.25 * dt
@@ -255,43 +264,62 @@
             return sums
 
         def farther(i):
-            return lax.rem(chip + 1 + lax.rem(chips // 2 - 1 + i, chips - 1), chips)
+            return lax.rem(chip + 1 + (chips // 2 - 1 + i) % (chips - 1), chips)
 
         def sib_copy(z, h):
             return copy_to(terms.at[step, 1 - core, z, h], sib_recv.at[step, z, h],
-                           sib_sems.at[step, 0, z, h], sib_sems.at[step, 1, z, h],
+                           sib_sems.at[step, 0, 0, 0], sib_sems.at[step, 1, z, h],
                            (me_space, sibling))
 
         def rs_copy(z, h):
-            return copy_to(terms.at[step, core, z, h], rs_recv.at[step, chip, h],
-                           rs_sems.at[step, 0, z, h], rs_sems.at[step, 1, chip, h],
+            slot = lax.rem(z + chips - 1 - chip, chips)
+            return copy_to(terms.at[step, core, z, h], rs_recv.at[step, h, slot],
+                           rs_sems.at[step, 0, 0], rs_sems.at[step, 1, h],
                            (me_space, 2 * z + core))
 
-        def rs_arrival(z, h):
-            return copy_to(terms.at[step, core, z, h], rs_recv.at[step, z, h],
-                           rs_sems.at[step, 0, z, h], rs_sems.at[step, 1, z, h],
-                           (me_space, 2 * z + core))
+        def rs_all(h):
+            return copy_to(rs_recv.at[step, h], rs_recv.at[step, h], rs_sems.at[step, 0, 0],
+                           rs_sems.at[step, 1, h], (me_space, sibling))
+
+        def rs_sent():
+            return copy_to(rs_recv.at[step], rs_recv.at[step], rs_sems.at[step, 0, 0],
+                           rs_sems.at[step, 1, 0], (me_space, sibling))
+
+        def sib_sent():
+            held = terms.at[step, 1 - core]
+            return copy_to(held, held, sib_sems.at[step, 0, 0, 0], sib_sems.at[step, 1, 0, 0],
+                           (me_space, sibling))
+
+        def ag_sent():
+            held = gnew.at[step, pl.ds(0, chips - 1)]
+            return copy_to(held, held, ag_sems.at[step, 0, 0, 0], ag_sems.at[step, 1, 0, 0],
+                           (me_space, sibling))
+
+        def fw_sent():
+            held = gnew.at[step, pl.ds(0, chips)]
+            return copy_to(held, held, fw_sems.at[step, 0, 0, 0], fw_sems.at[step, 1, 0, 0],
+                           (me_space, sibling))
 
         def ag_copy(z, h):
-            return copy_to(gnew.at[step, me, h], gnew.at[step, me, h], ag_sems.at[step, 0, z, h],
+            return copy_to(gnew.at[step, me, h], gnew.at[step, me, h], ag_sems.at[step, 0, 0, 0],
                            ag_sems.at[step, 1, chip, h], (me_space, 2 * z + core))
 
         def ag_arrival(z, h):
             there = 2 * z + core
             return copy_to(gnew.at[step, there, h], gnew.at[step, there, h],
-                           ag_sems.at[step, 0, z, h], ag_sems.at[step, 1, z, h],
+                           ag_sems.at[step, 0, 0, 0], ag_sems.at[step, 1, z, h],
                            (me_space, there))
 
         def fw_copy(z, h):
             there = 2 * z + core
             return copy_to(gnew.at[step, there, h], gnew.at[step, there, h],
-                           fw_sems.at[step, 0, z, h], fw_sems.at[step, 1, z, h],
+                           fw_sems.at[step, 0, 0, 0], fw_sems.at[step, 1, z, h],
                            (me_space, sibling))
 
         def fw_arrival(z, h):
             there = 2 * z + 1 - core
             return copy_to(gnew.at[step, there, h], gnew.at[step, there, h],
-                           fw_sems.at[step, 0, z, h], fw_sems.at[step, 1, z, h],
+                           fw_sems.at[step, 0, 0, 0], fw_sems.at[step, 1, z, h],
                            (me_space, sibling))
 
         own = []
@@ -306,7 +334,7 @@
                 for_sibling(farther(i))
                 return carry
 
-            lax.fori_loop(0, chips - 1, for_sibling_step, 0)
+            loop(chips - 1, for_sibling_step, 0)
             for_sibling(chip)
 
             def for_peers(i, carry):
@@ -318,7 +346,7 @@
                 rs_copy(z, h).start()
                 return carry
 
-            lax.fori_loop(0, chips - 1, for_peers, 0)
+            loop(chips - 1, for_peers, 0)
             own.append(drag(me, h))
 
         if step + 1 < STEPS:
@@ -327,14 +355,10 @@
         for h in range(halves):
             sib_copy(chip, h).wait_recv()
 
-            def gather_sums(i, sums):
-                z = lax.rem(chip + 1 + i, chips)
-                rs_arrival(z, h).wait_recv()
-                return tuple(sums[part] + rs_recv[step, z, h, part] for part in range(3))
-
-            sums = lax.fori_loop(
-                0, chips - 1, gather_sums,
-                tuple(own[h][part] + sib_recv[step, chip, h, part] for part in range(3)))
+            sums = [own[h][part] + sib_recv[step, chip, h, part] for part in range(3)]
+            rs_all(h).wait_recv()
+            for i in range(chips - 1):
+                sums = [sums[part] + rs_recv[step, h, i, part] for part in range(3)]
             rows, inner, cols = place(me, h)
             inverse = 1.0 / (1.0 + sums[0])
             gnew[step, me, h, 0] = (
@@ -346,7 +370,7 @@
                 ag_copy(farther(i), h).start()
                 return carry
 
-            lax.fori_loop(0, chips - 1, start_ag, 0)
+            loop(chips - 1, start_ag, 0)
             fw_copy(chip, h).start()
 
         def update(chunk, h, best):
@@ -377,51 +401,25 @@
                 fw_copy(z, h).start()
                 return update(2 * z + core, h, best)
 
-            top = lax.fori_loop(0, chips - 1, update_peer, top)
+            top = loop(chips - 1, update_peer, top)
 
             def update_sibling(i, best):
                 z = lax.rem(chip + i, chips)
                 fw_arrival(z, h).wait_recv()
                 return update(2 * z + 1 - core, h, best)
 
-            top = lax.fori_loop(0, chips, update_sibling, top)
-
-        unsent.append((top_copy_one, top_copy_two, sib_copy, rs_copy, ag_copy, fw_copy,
-                       rho_halos(step) + azi_halos(step)))
+            top = loop(chips, update_sibling, top)
+
+        unsent.append((top_all_one(), top_all_two(), sib_sent(), rs_sent(), ag_sent(), fw_sent(),
+                       *rho_halos(step), *azi_halos(step)))
         return top
 
     for step in range(STEPS):
         top = run_step(step, top)
 
-    for top_copy_one, top_copy_two, sib_copy, rs_copy, ag_copy, fw_copy, halos in unsent:
-
-        def sent_one(i, carry):
-            top_copy_one(i).wait_send()
-            return carry
-
-        def sent_two(i, carry):
-            top_copy_two(i).wait_send()
-            return carry
-
-        def sent_core(i, carry):
-            for h in range(halves):
-                sib_copy(i, h).wait_send()
-                fw_copy(i, h).wait_send()
-            return carry
-
-        def sent_chip(i, carry):
-            z = lax.rem(chip + 1 + i, chips)
-            for h in range(halves):
-                rs_copy(z, h).wait_send()
-                ag_copy(z, h).wait_send()
-            return carry
-
-        lax.fori_loop(0, m - 1, sent_one, 0)
-        lax.fori_loop(0, n - 1, sent_two, 0)
-        lax.fori_loop(0, chips, sent_core, 0)
-        lax.fori_loop(0, chips - 1, sent_chip, 0)
-        for halo in halos:
-            halo.wait_send()
+    for sends in unsent:
+        for send in sends:
+            send.wait_send()
 
 
 def finish(rho, rad, azi, damp, dust_out, gas_out, new, sems):
@@ -483,20 +481,20 @@
                 pltpu.VMEM((STEPS, 2, chips, halves, 3, 8, span), f32),
                 pltpu.VMEM((STEPS, n, halves, 2, 8, span), f32),
                 pltpu.VMEM((STEPS, chips, halves, 3, 8, span), f32),
-                pltpu.VMEM((STEPS, chips, halves, 3, 8, span), f32),
+                pltpu.VMEM((STEPS, halves, chips - 1, 3, 8, span), f32),
                 pltpu.VMEM((STEPS, 8, 128), f32),
-                pltpu.VMEM((STEPS, m, 8, 128), f32),
+                pltpu.VMEM((STEPS, m - 1, 8, 128), f32),
                 pltpu.VMEM((STEPS, 8, 128), f32),
-                pltpu.VMEM((STEPS, n, 8, 128), f32),
+                pltpu.VMEM((STEPS, n - 1, 8, 128), f32),
                 pltpu.VMEM((STEPS, 2, rho_rows, cells), f32),
                 pltpu.VMEM((STEPS, 2, rho_rows, cells), f32),
                 pltpu.VMEM((STEPS, 2, azi_rows, cells), f32),
                 pltpu.VMEM((STEPS, 2, azi_rows, cells), f32),
                 dma((7,)),
-                dma((STEPS, 4, max(n, m))),
+                dma((STEPS, 4)),
                 dma((STEPS, 4, 2)),
                 dma((STEPS, 2, chips, halves)),
-                dma((STEPS, 2, chips, halves)),
+                dma((STEPS, 2, halves)),
                 dma((STEPS, 2, chips, halves)),
                 dma((STEPS, 2, chips, halves)),
             ],

time: 47.1 us -> 46.3 us (0.983)
  Pallas kernels: 46.1 us -> 45.6 us
    pallas_call x1, Pallas kernels: 44.8 us -> 44.2 us  [local(): pl.pallas_call(functools.partial(kernel, n, m), out_shape=(extended, exte...]
where the time goes in v4:
time: 46.3 us; the launch traced here: 46.2 us
  Pallas kernels  45.6 us (98%)
  between operations  0.64 us (1%)
    pallas_call x1, Pallas kernels, local(): pl.pallas_call(functools.partial(kernel, n, m), out_shape=(extended, exte...  44.2 us
    pallas_call x1, Pallas kernels, local(): pl.pallas_call(finish, out_shape=(jax.ShapeDtypeStruct(dust_state.shape,...  1.36 us

profile of v4, /device:TPU:0, one launch (start us, length us, event | category | flops | bytes accessed | tf_op | source)
XLA Modules:
  0.0 46.2 jit_solution(6057912202254608373)
XLA Ops:
  0.6 44.2 %disk_steps.1 = (f32[5,48,1024]{2,1,0:T(8,128)S(1)}, f32[5,48,1024]{2,1,0:T(8,128)S(1)}, f32[5,48,1024]{2,1,0:T(8,128)S(1)}, f32[4,32,1024]{2,1,0:T(8,128)S(1)}) custom-call(f32[3,4,32,1024]{3,2,1,0:T(8,128)} %dust.1, f32[3,32,1024]{2,1,0:T(8,128)} %gas.1, s32[4]{0:T(128)} %species_bins.1), custom_call_target="tpu_custom_call" | custom-call | flops 32768000 | bytes 3932160 | tf_op jit(solution)/shard_map/disk_steps/pallas_call | solution.py:472
  44.8 1.4 %last_update.1 = (f32[3,4,32,1024]{3,2,1,0:T(8,128)}, f32[3,32,1024]{2,1,0:T(8,128)}) custom-call(f32[5,48,1024]{2,1,0:T(8,128)S(1)} %get-tuple-element.6.rho, f32[5,48,1024]{2,1,0:T(8,128)S(1)} %get-tuple-element.7.rad, f32[5,48,1024]{2,1,0:T(8,128)S(1)} %get-tuple-element.8.azi, f32[4,32,1024]{2,1,0:T(8,128)S(1)} %get-tuple-element.9.damp), custom_call_target="tpu_custom_call" | custom-call | tf_op jit(solution)/shard_map/last_update/pallas_call | solution.py:508

commit v5 on v4

--- a/solution.py
+++ b/solution.py
@@ -182,24 +182,26 @@
                 div[f, 8 * r:8 * r + 8, :] = flux - before
             return carry
 
-        lax.fori_loop(0, fluids, radial, 0)
-
+        early = fluids * 2 // 5
+        lax.fori_loop(0, early, radial, 0)
+
+        top_all_one().wait_recv()
+        for i in range(m - 1):
+            top = jnp.maximum(top, top_one[step, i])
+        top_mid[step] = top
+
+        def start_two(i, carry):
+            top_copy_two(i).start()
+            return carry
+
+        loop(n - 1, start_two, 0)
+
+        lax.fori_loop(early, fluids, radial, 0)
         for r in range(groups):
             here = rho[gas_at, TOP + 8 * r:TOP + 8 * r + 8, :]
             up = jnp.where(lanes < cells - 1, pltpu.roll(here, cells - 1, 1), here)
             low = jnp.where(lanes >= 1, pltpu.roll(here, 1, 1), here)
             push[0, 8 * r:8 * r + 8, :] = (up - low) * (0.5 / here)
-
-        top_all_one().wait_recv()
-        for i in range(m - 1):
-            top = jnp.maximum(top, top_one[step, i])
-        top_mid[step] = top
-
-        def start_two(i, carry):
-            top_copy_two(i).start()
-            return carry
-
-        loop(n - 1, start_two, 0)
 
         for halo in azi_halos(step) + rho_halos(step):
             halo.wait_recv()

time: 46.3 us -> 46.3 us (level)
  no operation moved by 1% of the time
where the time goes in v5:
time: 46.3 us; the launch traced here: 46.2 us
  Pallas kernels  45.6 us (98%)
  between operations  0.64 us (1%)
    pallas_call x1, Pallas kernels, local(): pl.pallas_call(functools.partial(kernel, n, m), out_shape=(extended, exte...  44.2 us
    pallas_call x1, Pallas kernels, local(): pl.pallas_call(finish, out_shape=(jax.ShapeDtypeStruct(dust_state.shape,...  1.36 us

profile of v5, /device:TPU:0, one launch (start us, length us, event | category | flops | bytes accessed | tf_op | source)
XLA Modules:
  0.0 46.2 jit_solution(14381518915449564711)
XLA Ops:
  0.6 44.2 %disk_steps.1 = (f32[5,48,1024]{2,1,0:T(8,128)S(1)}, f32[5,48,1024]{2,1,0:T(8,128)S(1)}, f32[5,48,1024]{2,1,0:T(8,128)S(1)}, f32[4,32,1024]{2,1,0:T(8,128)S(1)}) custom-call(f32[3,4,32,1024]{3,2,1,0:T(8,128)} %dust.1, f32[3,32,1024]{2,1,0:T(8,128)} %gas.1, s32[4]{0:T(128)} %species_bins.1), custom_call_target="tpu_custom_call" | custom-call | flops 32768000 | bytes 3932160 | tf_op jit(solution)/shard_map/disk_steps/pallas_call | solution.py:474
  44.8 1.4 %last_update.1 = (f32[3,4,32,1024]{3,2,1,0:T(8,128)}, f32[3,32,1024]{2,1,0:T(8,128)}) custom-call(f32[5,48,1024]{2,1,0:T(8,128)S(1)} %get-tuple-element.6.rho, f32[5,48,1024]{2,1,0:T(8,128)S(1)} %get-tuple-element.7.rad, f32[5,48,1024]{2,1,0:T(8,128)S(1)} %get-tuple-element.8.azi, f32[4,32,1024]{2,1,0:T(8,128)S(1)} %get-tuple-element.9.damp), custom_call_target="tpu_custom_call" | custom-call | tf_op jit(solution)/shard_map/last_update/pallas_call | solution.py:510

commit v6 on v5

--- a/solution.py
+++ b/solution.py
@@ -16,7 +16,7 @@
 
 MESH = pl.DeviceIdType.MESH
 TOP = 8
-HALVES = 1
+HALVES = 2
 
 
 def loop(count, body, carry):

time: 46.3 us -> 45.9 us (level)
  Pallas kernels: 45.6 us -> 45.1 us
    pallas_call x1, Pallas kernels: 44.2 us -> 43.7 us  [local(): pl.pallas_call(functools.partial(kernel, n, m), out_shape=(extended, exte...]
where the time goes in v6:
time: 45.9 us; the launch traced here: 45.7 us
  Pallas kernels  45.1 us (98%)
  between operations  0.64 us (1%)
    pallas_call x1, Pallas kernels, local(): pl.pallas_call(functools.partial(kernel, n, m), out_shape=(extended, exte...  43.7 us
    pallas_call x1, Pallas kernels, local(): pl.pallas_call(finish, out_shape=(jax.ShapeDtypeStruct(dust_state.shape,...  1.36 us

profile of v6, /device:TPU:0, one launch (start us, length us, event | category | flops | bytes accessed | tf_op | source)
XLA Modules:
  0.0 45.7 jit_solution(7169613818685966996)
XLA Ops:
  0.6 43.7 %disk_steps.1 = (f32[5,48,1024]{2,1,0:T(8,128)S(1)}, f32[5,48,1024]{2,1,0:T(8,128)S(1)}, f32[5,48,1024]{2,1,0:T(8,128)S(1)}, f32[4,32,1024]{2,1,0:T(8,128)S(1)}) custom-call(f32[3,4,32,1024]{3,2,1,0:T(8,128)} %dust.1, f32[3,32,1024]{2,1,0:T(8,128)} %gas.1, s32[4]{0:T(128)} %species_bins.1), custom_call_target="tpu_custom_call" | custom-call | flops 32768000 | bytes 3932160 | tf_op jit(solution)/shard_map/disk_steps/pallas_call | solution.py:474
  44.3 1.4 %last_update.1 = (f32[3,4,32,1024]{3,2,1,0:T(8,128)}, f32[3,32,1024]{2,1,0:T(8,128)}) custom-call(f32[5,48,1024]{2,1,0:T(8,128)S(1)} %get-tuple-element.6.rho, f32[5,48,1024]{2,1,0:T(8,128)S(1)} %get-tuple-element.7.rad, f32[5,48,1024]{2,1,0:T(8,128)S(1)} %get-tuple-element.8.azi, f32[4,32,1024]{2,1,0:T(8,128)S(1)} %get-tuple-element.9.damp), custom_call_target="tpu_custom_call" | custom-call | tf_op jit(solution)/shard_map/last_update/pallas_call | solution.py:510
